TPU v7x, 128 devices: a whole 4x4x4 slice. The times are simulated.
128 devices in a mesh: ta: 2 (over y_lo), ha: 64 (over y_hi, z, x, core).
Axes of the slice: x: 4, y: 4 (y_hi: 2, y_lo: 2; y = y_hi * 2 + y_lo), z: 4, core: 2. Of those that a mesh axis runs over, the one named last changes fastest.
Arguments:
- tokens: bfloat16 [4, 128, 10240], P(None, 'ha', 'ta'), may hold values from -6 to 6
- cache_latent: bfloat16 [2, 256, 5120], P(None, 'ha'), may hold values from -6 to 6
- cache_feature: bfloat16 [2, 512, 640, 192], P(None, 'ha'), may hold values from -0.25 to 2
- weight_in: bfloat16 [3, 3, 3, 16, 384], replicated, may hold values from -0.3125 to 0.3125
- weight_up: bfloat16 [3, 3, 384, 192], replicated, may hold values from -0.109375 to 0.109375
- weight_out: bfloat16 [3, 3, 3, 18432], replicated, may hold values from -0.078125 to 0.078125
- weight_skip: bfloat16 [192, 96], replicated, may hold values from -0.4375 to 0.4375
- bias_in: float32 [384], replicated, may hold values from -3 to 3
- bias_up: float32 [192], replicated, may hold values from -3 to 3
- bias_out: float32 [96], replicated, may hold values from -3 to 3
- gain_in: float32 [384], replicated, may hold values from 0.1 to 1.9
- gain_up: float32 [192], replicated, may hold values from 0.1 to 1.9
Outputs:
- decoded: bfloat16 [4, 512, 61440], P('ta', 'ha')
All inputs are finite; a program needn't handle non-finite values.
Results may differ from a plain program's by a relative error of at most 0.0051.
Values may be sent and summed in bfloat16 or wider, within the bound.
A program may use at most 128 MiB of HBM per device.

v0:
```python
import jax
import jax.numpy as jnp
from jax import lax
from jax.sharding import PartitionSpec as P

C0 = 16
C2 = 192
C3 = 96
ROWS = 4
WL = 320


def passed_along(value, axis, by):
    count = lax.axis_size(axis)
    pairs = [(i, i + by) for i in range(count) if 0 <= i + by < count]
    return lax.ppermute(value, axis, pairs)


def padded(block, sides, width):
    for axis, dim in sides:
        count = lax.axis_size(axis)
        forward = [(i, i + 1) for i in range(count - 1)]
        backward = [(target, source) for source, target in forward]
        low = lax.ppermute(
            lax.slice_in_dim(block, block.shape[dim] - width, None, axis=dim), axis, forward
        )
        high = lax.ppermute(lax.slice_in_dim(block, 0, width, axis=dim), axis, backward)
        block = jnp.concatenate([low, block, high], axis=dim)
    return block


def normed(field, gain):
    scale = lax.rsqrt(jnp.mean(field * field, axis=-1, keepdims=True) + 1e-06)
    return jax.nn.silu(field * scale * gain)


def conv_time(field, kernel, col_pad):
    return lax.conv_general_dilated(
        field[None],
        kernel,
        (1, 1, 1),
        [(0, 0), (0, 0), (col_pad, col_pad)],
        dimension_numbers=("NDHWC", "DHWIO", "NDHWC"),
        preferred_element_type=jnp.float32,
    )[0]


def conv_plane(field, kernel, col_pad):
    return lax.conv_general_dilated(
        field,
        kernel,
        (1, 1),
        [(0, 0), (col_pad, col_pad)],
        dimension_numbers=("NHWC", "HWIO", "NHWC"),
        preferred_element_type=jnp.float32,
    )


def upsample(field):
    return jnp.repeat(jnp.repeat(field, 2, axis=1), 2, axis=2)


def shards(
    tokens,
    cache_latent,
    cache_feature,
    weight_in,
    weight_up,
    weight_out,
    weight_skip,
    bias_in,
    bias_up,
    bias_out,
    gain_in,
    gain_up,
):
    lat_width = 1
    local = lax.all_to_all(tokens, "ta", split_axis=0, concat_axis=2, tiled=True)
    frames = local.shape[0]
    patch_rows = local.shape[1]
    own_cols = WL
    col_pad = 1
    latent = (
        local.reshape(frames, patch_rows, WL // 2, 2, 2, C0)
        .transpose(0, 1, 3, 2, 4, 5)
        .reshape(frames, ROWS, WL, C0)
    )
    first_time = lax.axis_index("ta") == 0
    earlier = passed_along(latent, "ta", 1)
    earlier = jnp.where(first_time, cache_latent.reshape(2, ROWS, WL, C0), earlier)
    stacked = jnp.concatenate([earlier, latent], 0)
    volume = padded(stacked, (("ha", 1),), lat_width)
    first_map = conv_time(volume, weight_in, col_pad) + bias_in
    first_act = normed(first_map, gain_in).astype(jnp.bfloat16)
    up_width = 1
    lifted = padded(upsample(first_act), (("ha", 1),), up_width)
    second_map = conv_plane(lifted, weight_up, col_pad) + bias_up
    second_act = normed(second_map, gain_up).astype(jnp.bfloat16)
    skip_in = second_map.astype(jnp.bfloat16)
    feature_rows = padded(second_act, (("ha", 1),), 1)
    cached = padded(cache_feature, (("ha", 1),), 1)
    previous = passed_along(feature_rows[-2:], "ta", 1)
    previous = jnp.where(first_time, cached, previous)
    window = jnp.concatenate([previous, feature_rows], 0)
    main = conv_time(window, weight_out.reshape(3, 3, 3, C2, C3), col_pad)
    skipped = jnp.einsum("fhwc,cd->fhwd", skip_in, weight_skip, preferred_element_type=jnp.float32)
    decoded = (main + bias_out + skipped).astype(jnp.bfloat16)
    decoded = decoded.reshape(frames, 2 * ROWS, 2 * own_cols * C3)
    return decoded


def solution(mesh):
    placed = (
        P(None, "ha", "ta"),
        P(None, "ha", None),
        P(None, "ha", None, None),
        P(),
        P(),
        P(),
        P(),
        P(),
        P(),
        P(),
        P(),
        P(),
    )
    return jax.shard_map(
        shards, mesh=mesh, in_specs=placed, out_specs=P("ta", "ha", None), check_vma=False
    )
```

profile of v0, /device:TPU:24, one launch (start us, length us, event | category | flops | bytes accessed | tf_op | source)
XLA Modules:
  0.0 406.5 jit_solution(9864111470767588708)
XLA Ops:
  0.0 6.4 %all_to_all.15 = bf16[4,2,5120]{2,1,0:T(2,128)(2,1)S(1)} all-to-all(bf16[4,2,5120]{2,1,0:T(2,128)(2,1)} %param.12), channel_id=1, replica_groups=mesh['ta'=2,'ha'=64] {'ta'}, dimensions={0} | all-to-all | bytes 163840 | tf_op jit(solution)/shard_map/all_to_all | solution.py:78
  10.4 3.8 collective-permute-done.2
  14.9 1.9 collective-permute-start.3
  16.8 9.4 %collective-permute-start.4 = (bf16[4,1,320,16]{2,3,1,0:T(8,128)(2,1)S(1)}, bf16[4,1,320,16]{2,3,1,0:T(8,128)(2,1)S(1)}, u32[]{:S(2)}, u32[]{:S(2)}) collective-permute-start(bf16[4,1,320,16]{2,3,1,0:T(8,128)(2,1)S(1)} %get-tuple-element.14), channel_id=1, source_target_pairs={{1,0},{2,1},{3,2},{4,3},{5,4},{6,5},{7,6},{8,7},{9,8},{10,9},{11,1... | collective-permute-start | bytes 122888 | tf_op jit(solution)/shard_map/ppermute | solution.py:27
  26.2 1.7 collective-permute-done.4
  28.9 2.8 copy.120
  32.6 4.3 %fusion.29 = f32[2,4,8,41,384]{4,2,3,1,0:T(8,128)S(1)} fusion(bf16[3,3,3,16,384]{4,3,2,1,0:T(8,128)(2,1)} %param.15, bf16[4,6,1,7,2,16]{5,3,4,1,0,2:T(8,128)(2,1)S(1)} %slice.40, bf16[4,6,1,8,41,16]{5,3,4,1,0,2:T(8,128)(2,1)} %copy.120, pred[8,41]{0,1:T(8,128)(4,1)S(1)} %copy-done.14), kind=kOutput, calls=%fused_computation.39 | convolution fusion | flops 872380416 | bytes 4625224 | tf_op jit(solution)/shard_map/conv_general_dilated | solution.py:38
  40.5 2.0 copy.123
  42.5 3.9 broadcast_in_dim.9
  46.4 5.7 %broadcast_in_dim.10 = bf16[2,8,320,2,384]{4,0,3,2,1:T(2,128)(2,1)S(1)} broadcast(bf16[2,8,320,384]{3,0,2,1:T(2,128)(2,1)} %bitcast.87), dimensions={0,1,2,4} | broadcast | bytes 11796480 | tf_op jit(solution)/shard_map/broadcast_in_dim | solution.py:60
  53.5 1.9 collective-permute-start.5
  55.4 9.4 %collective-permute-start.6 = (bf16[2,1,640,384]{3,0,2,1:T(2,128)(2,1)S(1)}, bf16[2,1,640,384]{3,0,2,1:T(2,128)(2,1)S(1)}, u32[]{:S(2)}, u32[]{:S(2)}) collective-permute-start(bf16[2,1,640,384]{3,0,2,1:T(2,128)(2,1)S(1)} %get-tuple-element.8), channel_id=1, source_target_pairs={{1,0},{2,1},{3,2},{4,3},{5,4},{6,5},{7,6},{8,7},{9,8},{10,9},{11,1... | collective-permute-start | bytes 2949128 | tf_op jit(solution)/shard_map/ppermute | solution.py:27
  64.8 9.8 %collective-permute-done.5 = bf16[2,1,640,384]{3,0,2,1:T(2,128)(2,1)S(1)} collective-permute-done((bf16[2,1,640,384]{3,0,2,1:T(2,128)(2,1)S(1)}, bf16[2,1,640,384]{3,0,2,1:T(2,128)(2,1)S(1)}, u32[]{:S(2)}, u32[]{:S(2)}) %collective-permute-start.5) | collective-permute-done | bytes 983072 | tf_op jit(solution)/shard_map/ppermute | solution.py:24
  74.7 1.8 collective-permute-done.6
  76.4 17.1 %maximum_bitcast_fusion = bf16[10,2,640,384]{3,1,2,0:T(2,128)(2,1)S(1)} fusion(bf16[2,1,640,384]{3,0,2,1:T(2,128)(2,1)S(1)} %collective-permute-done.6, bf16[2,8,640,384]{3,0,2,1:T(2,128)(2,1)S(1)} %bitcast.83, bf16[2,1,640,384]{3,0,2,1:T(2,128)(2,1)S(1)} %collective-permute-done.5), kind=kLoop, calls=%fused_computation.19 | loop fusion | flops 9830400 | bytes 19660800 | tf_op jit(solution)/shard_map/concatenate | solution.py:28
  93.5 8.5 %pad.2 = bf16[10,2,648,384]{3,1,2,0:T(2,128)(2,1)S(1)} pad(bf16[10,2,640,384]{3,1,2,0:T(2,128)(2,1)S(1)} %maximum_bitcast_fusion, bf16[]{:T(256)} %constant.27), padding=0_0x0_0x1_7x0_0 | pad | bytes 19783682 | tf_op jit(solution)/shard_map/concatenate | solution.py:28
  102.2 9.6 %fusion.10 = bf16[10,2,8,83,384]{4,1,3,2,0:T(2,128)(2,1)S(1)} fusion(bf16[10,2,7,2,384]{4,1,3,2,0:T(2,128)(2,1)S(1)} %slice.44, bf16[10,2,8,81,384]{4,1,3,2,0:T(2,128)(2,1)S(1)} %bitcast.81), kind=kLoop, calls=%fused_computation.15 | loop fusion | flops 30597120 | bytes 20367360 | tf_op jit(solution)/shard_map/conv_general_dilated | solution.py:49
  111.8 24.9 %fusion.45 = (bf16[8,16,81,192]{3,1,2,0:T(8,128)(2,1)}, f32[8,16,81]{1,2,0:T(8,128)S(1)}, f32[8,16,81,192]{3,1,2,0:T(8,128)}) fusion(f32[192]{0:T(256)S(1)} %copy-done.11, bf16[3,3,384,192]{2,3,1,0:T(8,128)(2,1)S(1)} %copy-done, bf16[10,2,8,83,384]{4,1,3,2,0:T(2,128)(2,1)S(1)} %fusion.10, pred[16,81]{0,1:T(8,128)(4,1)S(1)} %copy-done.13), kind=kOutput, calls=%fused_computation.59 | convolution fusion | flops 13769357312 | bytes 23513616 | tf_op jit(solution)/shard_map/conv_general_dilated | solution.py:49
  137.3 10.2 %copy.125 = f32[8,16,81,192]{3,0,2,1:T(8,128)S(1)} copy(f32[8,16,81,192]{3,1,2,0:T(8,128)} %get-tuple-element.15) | data formatting | bytes 15925248 | tf_op jit(solution)/shard_map/add | solution.py:97
  147.5 4.6 %multiply_convert_fusion = bf16[2,8,640,192]{3,1,2,0:T(8,128)(2,1)} fusion(f32[8,2,648,192]{3,0,2,1:T(8,128)S(1)} %bitcast.79, f32[192]{0:T(256)S(1)} %copy-done.10, f32[2,8,640]{1,2,0:T(8,128)S(1)} %copy.127), kind=kLoop, calls=%fused_computation.14 | loop fusion | flops 13762560 | bytes 11838208 | tf_op jit(solution)/shard_map/convert_element_type | solution.py:98
  152.1 6.1 %fusion.47 = (bf16[2,1,640,192]{3,1,2,0:T(2,128)(2,1)S(1)}, bf16[2,1,640,192]{3,1,2,0:T(2,128)(2,1)S(1)}) fusion(bf16[2,8,640,192]{3,1,2,0:T(8,128)(2,1)} %multiply_convert_fusion), kind=kLoop, calls=%fused_computation.61 | loop fusion | bytes 1966080 | tf_op jit(solution)/shard_map/slice | solution.py:25
  158.2 1.9 copy.128
  160.1 2.5 copy.129
  162.6 9.5 %collective-permute-start.8 = (bf16[2,1,640,192]{2,3,1,0:T(8,128)(2,1)}, bf16[2,1,640,192]{2,3,1,0:T(8,128)(2,1)S(1)}, u32[]{:S(2)}, u32[]{:S(2)}) collective-permute-start(bf16[2,1,640,192]{2,3,1,0:T(8,128)(2,1)} %copy.129), channel_id=1, source_target_pairs={{1,0},{2,1},{3,2},{4,3},{5,4},{6,5},{7,6},{8,7},{9,8},{10,9},{11,1... | collective-permute-start | bytes 1474568 | tf_op jit(solution)/shard_map/ppermute | solution.py:27
  172.2 1.9 collective-permute-start.7
  174.1 8.5 %copy.130 = bf16[2,8,640,192]{2,3,1,0:T(8,128)(2,1)} copy(bf16[2,8,640,192]{3,1,2,0:T(8,128)(2,1)} %multiply_convert_fusion) | data formatting | bytes 7864320 | tf_op jit(solution)/shard_map/convert_element_type | solution.py:98
  182.5 5.5 %collective-permute-done.7 = bf16[2,1,640,192]{2,3,1,0:T(8,128)(2,1)S(1)} collective-permute-done((bf16[2,1,640,192]{2,3,1,0:T(8,128)(2,1)S(1)}, bf16[2,1,640,192]{2,3,1,0:T(8,128)(2,1)S(1)}, u32[]{:S(2)}, u32[]{:S(2)}) %collective-permute-start.7) | collective-permute-done | bytes 491552 | tf_op jit(solution)/shard_map/ppermute | solution.py:24
  188.0 5.0 %pad_maximum_fusion = bf16[2,10,640,192]{2,3,1,0:T(8,128)(2,1)} fusion(bf16[2,1,640,192]{2,3,1,0:T(8,128)(2,1)S(1)} %collective-permute-done.8, bf16[2,8,640,192]{2,3,1,0:T(8,128)(2,1)} %copy.130, bf16[2,1,640,192]{2,3,1,0:T(8,128)(2,1)S(1)} %collective-permute-done.7), kind=kLoop, calls=%fused_computation.23 | loop fusion | flops 4915200 | bytes 9830400 | tf_op jit(solution)/shard_map/concatenate | solution.py:28
  194.5 2.2 fusion.48
  196.8 1.9 collective-permute-start
  198.7 9.4 %collective-permute-start.1 = (bf16[2,1,640,192]{2,3,1,0:T(8,128)(2,1)}, bf16[2,1,640,192]{2,3,1,0:T(8,128)(2,1)}, u32[]{:S(2)}, u32[]{:S(2)}) collective-permute-start(bf16[2,1,640,192]{2,3,1,0:T(8,128)(2,1)} %get-tuple-element.12), channel_id=1, source_target_pairs={{1,0},{2,1},{3,2},{4,3},{5,4},{6,5},{7,6},{8,7},{9,8},{10,9},{11,1... | collective-permute-start | bytes 1474568 | tf_op jit(solution)/shard_map/ppermute | solution.py:27
  208.1 2.3 reshape.48
  210.4 4.4 %copy.136 = bf16[8,16,81,192]{3,0,2,1:T(8,128)(2,1)S(1)} copy(bf16[8,16,81,192]{3,1,2,0:T(8,128)(2,1)} %get-tuple-element.5) | data formatting | bytes 7962624 | tf_op jit(solution)/shard_map/convert_element_type | solution.py:99
  214.7 2.7 slice.51
  217.4 8.5 %copy.144 = bf16[8,2,640,192]{2,3,0,1:T(8,128)(2,1)} copy(bf16[8,2,640,192]{3,0,2,1:T(8,128)(2,1)} %slice.51) | data formatting | bytes 7864320
  225.9 65.1 %collective-permute-done.9 = bf16[2,10,640,192]{2,3,1,0:T(8,128)(2,1)} collective-permute-done((bf16[2,10,640,192]{2,3,1,0:T(8,128)(2,1)}, bf16[2,10,640,192]{2,3,1,0:T(8,128)(2,1)}, u32[]{:S(2)}, u32[]{:S(2)}) %collective-permute-start.9) | collective-permute-done | bytes 4915232 | tf_op jit(solution)/shard_map/ppermute | solution.py:16
  291.1 4.5 %maximum_select_fusion = bf16[2,10,640,192]{2,3,1,0:T(8,128)(2,1)S(1)} fusion(bf16[2,10,640,192]{2,3,1,0:T(8,128)(2,1)} %collective-permute-done.9, bf16[2,1,640,192]{2,3,1,0:T(8,128)(2,1)} %collective-permute-done.1, bf16[2,8,640,192]{2,3,1,0:T(8,128)(2,1)} %param.14, bf16[2,1,640,192]{2,3,1,0:T(8,128)(2,1)S(1)} %collective-permute-done, pred[]{:T(512)S(6)} %eq.3), kind=kLoop, calls=%fused_computation.22 | loop fusion | flops 7372800 | bytes 14745601 | tf_op jit(solution)/shard_map/jit(_where)/select_n | solution.py:103
  295.6 5.0 %maximum_bitcast_fusion.1 = bf16[4,10,1,640,192]{3,4,1,0,2:T(8,128)(2,1)} fusion(bf16[2,1,640,192]{2,3,1,0:T(8,128)(2,1)S(1)} %collective-permute-done.8, bf16[2,8,640,192]{2,3,1,0:T(8,128)(2,1)S(1)} %copy-done.2, bf16[2,1,640,192]{2,3,1,0:T(8,128)(2,1)S(1)} %collective-permute-done.7, bf16[2,10,640,192]{2,3,1,0:T(8,128)(2,1)S(1)} %maximum_select_fusion), kind=kLoop, calls=%fused_computation.20 | loop fusion | flops 14745600 | bytes 19660800 | tf_op jit(solution)/shard_map/broadcast_in_dim | solution.py:39
  300.6 20.3 %copy.145 = bf16[4,10,1,640,192]{4,0,3,1,2:T(4,128)(2,1)} copy(bf16[4,10,1,640,192]{3,4,1,0,2:T(8,128)(2,1)} %maximum_bitcast_fusion.1) | data formatting | bytes 19660800
  320.9 8.7 %pad.4.clone = bf16[4,10,1,648,192]{4,0,3,1,2:T(4,128)(2,1)S(1)} pad(bf16[4,10,1,640,192]{4,0,3,1,2:T(4,128)(2,1)} %copy.145, bf16[]{:T(256)} %constant.27), padding=0_0x0_0x0_0x1_7x0_0 | pad | bytes 19783682 | tf_op jit(solution)/shard_map/broadcast_in_dim | solution.py:39
  329.6 10.7 %copy.133 = bf16[4,10,1,8,81,192]{5,3,4,1,0,2:T(8,128)(2,1)S(1)} copy(bf16[4,10,1,8,81,192]{5,0,4,3,1,2:T(4,128)(2,1)S(1)} %bitcast.78) | data formatting | bytes 19906560 | tf_op jit(solution)/shard_map/conv_general_dilated | solution.py:38
  340.3 4.7 %copy-done.3 = bf16[4,10,1,8,81,192]{5,3,4,1,0,2:T(8,128)(2,1)} copy-done((bf16[4,10,1,8,81,192]{5,3,4,1,0,2:T(8,128)(2,1)}, bf16[4,10,1,8,81,192]{5,3,4,1,0,2:T(8,128)(2,1)S(1)}, u32[]{:S(2)}) %copy-start.3) | copy-done | bytes 9953304
  345.1 38.2 %broadcast_select_fusion = f32[2,8,8,81,96]{4,2,3,1,0:T(8,128)S(1)} fusion(pred[8,81]{0,1:T(8,128)(4,1)S(1)} %copy-done.12, bf16[3,3,3,192,96]{4,3,2,1,0:T(8,128)(2,1)S(1)} %copy-done.5, bf16[4,10,1,7,2,192]{5,3,4,1,0,2:T(8,128)(2,1)S(1)} %slice.49, bf16[4,10,1,8,81,192]{5,3,4,1,0,2:T(8,128)(2,1)} %copy-done.3), kind=kOutput, calls=%fused_computation.35 | convolution fusion | flops 10351153152 | bytes 15145608 | tf_op jit(solution)/shard_map/conv_general_dilated | solution.py:38
  384.4 2.7 slice.50
  387.1 5.9 %copy.143 = f32[2,8,1,640,96]{3,4,1,0,2:T(8,128)} copy(f32[2,8,1,640,96]{4,1,3,0,2:T(8,128)} %slice.50) | data formatting | bytes 7864320
  393.1 4.4 %fusion.22 = bf16[2,8,640,96]{2,3,1,0:T(8,128)(2,1)S(1)} fusion(f32[2,8,1,640,96]{3,4,1,0,2:T(8,128)} %copy.143, bf16[8,2,640,192]{2,3,0,1:T(8,128)(2,1)} %copy.144, f32[96]{0:T(128)S(1)} %copy-done.9, bf16[192,96]{1,0:T(8,128)(2,1)S(1)} %copy-done.6), kind=kOutput, calls=%fused_computation.32 | convolution fusion | flops 380436480 | bytes 9867648 | tf_op jit(solution)/shard_map/fhwc,cd->fhwd/dot_general | solution.py:106
  397.4 2.6 copy.139
  400.0 6.0 %reshape.49 = bf16[2,8,61440]{2,1,0:T(8,128)(2,1)} reshape(bf16[2,8,640,96]{3,2,1,0:T(8,128)(2,1)} %copy.139) | data formatting | bytes 3932160 | tf_op jit(solution)/shard_map/reshape | solution.py:108
  (62 shorter events, 14.8 us)
Async XLA Ops:
  0.0 111.8 %copy-start = (bf16[3,3,384,192]{2,3,1,0:T(8,128)(2,1)S(1)}, bf16[3,3,384,192]{2,3,1,0:T(8,128)(2,1)}, u32[]{:S(2)}) copy-start(bf16[3,3,384,192]{2,3,1,0:T(8,128)(2,1)} %param.16) | copy-start | bytes 3981316
  7.7 24.9 %copy-start.14 = (pred[8,41]{0,1:T(8,128)(4,1)S(1)}, pred[8,41]{0,1:T(8,128)(4,1)}, u32[]{:S(2)}) copy-start(pred[8,41]{0,1:T(8,128)(4,1)} %constant.41) | copy-start | bytes 988
  7.7 6.5 %collective-permute-start.2 = (bf16[2,4,320,16]{2,3,1,0:T(8,128)(2,1)S(1)}, bf16[2,4,320,16]{2,3,1,0:T(8,128)(2,1)S(1)}, u32[]{:S(2)}, u32[]{:S(2)}) collective-permute-start(bf16[2,4,320,16]{2,3,1,0:T(8,128)(2,1)S(1)} %copy.115), channel_id=1, source_target_pairs={{0,64},{1,65},{2,66},{3,67},{4,68},{5,69},{6,70},{7,71},{8,72},{9,... | collective-permute-start | bytes 245768 | tf_op jit(solution)/shard_map/ppermute | solution.py:16
  14.9 11.3 %collective-permute-start.3 = (bf16[4,1,320,16]{2,3,1,0:T(8,128)(2,1)S(1)}, bf16[4,1,320,16]{2,3,1,0:T(8,128)(2,1)S(1)}, u32[]{:S(2)}, u32[]{:S(2)}) collective-permute-start(bf16[4,1,320,16]{2,3,1,0:T(8,128)(2,1)S(1)} %get-tuple-element.13), channel_id=1, source_target_pairs={{0,1},{1,2},{2,3},{3,4},{4,5},{5,6},{6,7},{7,8},{8,9},{9,10},{10,1... | collective-permute-start | bytes 122888 | tf_op jit(solution)/shard_map/ppermute | solution.py:24
  16.8 11.1 %collective-permute-start.4 = (bf16[4,1,320,16]{2,3,1,0:T(8,128)(2,1)S(1)}, bf16[4,1,320,16]{2,3,1,0:T(8,128)(2,1)S(1)}, u32[]{:S(2)}, u32[]{:S(2)}) collective-permute-start(bf16[4,1,320,16]{2,3,1,0:T(8,128)(2,1)S(1)} %get-tuple-element.14), channel_id=1, source_target_pairs={{1,0},{2,1},{3,2},{4,3},{5,4},{6,5},{7,6},{8,7},{9,8},{10,9},{11,1... | collective-permute-start | bytes 122888 | tf_op jit(solution)/shard_map/ppermute | solution.py:27
  37.9 0.7 copy-start.7
  37.9 1.3 copy-start.8
  53.5 21.2 %collective-permute-start.5 = (bf16[2,1,640,384]{3,0,2,1:T(2,128)(2,1)S(1)}, bf16[2,1,640,384]{3,0,2,1:T(2,128)(2,1)S(1)}, u32[]{:S(2)}, u32[]{:S(2)}) collective-permute-start(bf16[2,1,640,384]{3,0,2,1:T(2,128)(2,1)S(1)} %get-tuple-element.7), channel_id=1, source_target_pairs={{0,1},{1,2},{2,3},{3,4},{4,5},{5,6},{6,7},{7,8},{8,9},{9,10},{10,1... | collective-permute-start | bytes 2949128 | tf_op jit(solution)/shard_map/ppermute | solution.py:24
  55.4 21.0 %collective-permute-start.6 = (bf16[2,1,640,384]{3,0,2,1:T(2,128)(2,1)S(1)}, bf16[2,1,640,384]{3,0,2,1:T(2,128)(2,1)S(1)}, u32[]{:S(2)}, u32[]{:S(2)}) collective-permute-start(bf16[2,1,640,384]{3,0,2,1:T(2,128)(2,1)S(1)} %get-tuple-element.8), channel_id=1, source_target_pairs={{1,0},{2,1},{3,2},{4,3},{5,4},{6,5},{7,6},{8,7},{9,8},{10,9},{11,1... | collective-permute-start | bytes 2949128 | tf_op jit(solution)/shard_map/ppermute | solution.py:27
  102.2 9.6 %copy-start.11 = (f32[192]{0:T(256)S(1)}, f32[192]{0:T(256)}, u32[]{:S(2)}) copy-start(f32[192]{0:T(256)} %param.20) | copy-start | bytes 2308
  102.2 9.6 %copy-start.13 = (pred[16,81]{0,1:T(8,128)(4,1)S(1)}, pred[16,81]{0,1:T(8,128)(4,1)}, u32[]{:S(2)}) copy-start(pred[16,81]{0,1:T(8,128)(4,1)} %constant.40) | copy-start | bytes 3892
  137.3 10.2 %copy-start.10 = (f32[192]{0:T(256)S(1)}, f32[192]{0:T(256)}, u32[]{:S(2)}) copy-start(f32[192]{0:T(256)} %param.23) | copy-start | bytes 2308
  162.6 19.9 %collective-permute-start.8 = (bf16[2,1,640,192]{2,3,1,0:T(8,128)(2,1)}, bf16[2,1,640,192]{2,3,1,0:T(8,128)(2,1)S(1)}, u32[]{:S(2)}, u32[]{:S(2)}) collective-permute-start(bf16[2,1,640,192]{2,3,1,0:T(8,128)(2,1)} %copy.129), channel_id=1, source_target_pairs={{1,0},{2,1},{3,2},{4,3},{5,4},{6,5},{7,6},{8,7},{9,8},{10,9},{11,1... | collective-permute-start | bytes 1474568 | tf_op jit(solution)/shard_map/ppermute | solution.py:27
  172.2 15.9 %collective-permute-start.7 = (bf16[2,1,640,192]{2,3,1,0:T(8,128)(2,1)S(1)}, bf16[2,1,640,192]{2,3,1,0:T(8,128)(2,1)S(1)}, u32[]{:S(2)}, u32[]{:S(2)}) collective-permute-start(bf16[2,1,640,192]{2,3,1,0:T(8,128)(2,1)S(1)} %copy.128), channel_id=1, source_target_pairs={{0,1},{1,2},{2,3},{3,4},{4,5},{5,6},{6,7},{7,8},{8,9},{9,10},{10,1... | collective-permute-start | bytes 1474568 | tf_op jit(solution)/shard_map/ppermute | solution.py:24
  182.5 25.5 %copy-start.4 = (bf16[3,3,3,18432]{3,2,1,0:T(4,128)(2,1)S(1)}, bf16[3,3,3,18432]{3,2,1,0:T(4,128)(2,1)}, u32[]{:S(2)}) copy-start(bf16[3,3,3,18432]{3,2,1,0:T(4,128)(2,1)} %param.17) | copy-start | bytes 2985988
  193.0 98.0 %collective-permute-start.9 = (bf16[2,10,640,192]{2,3,1,0:T(8,128)(2,1)}, bf16[2,10,640,192]{2,3,1,0:T(8,128)(2,1)}, u32[]{:S(2)}, u32[]{:S(2)}) collective-permute-start(bf16[2,10,640,192]{2,3,1,0:T(8,128)(2,1)} %pad_maximum_fusion), channel_id=1, source_target_pairs={{0,64},{1,65},{2,66},{3,67},{4,68},{5,69},{6,70},{7,71},{8,72},{9,... | collective-permute-start | bytes 14745608 | tf_op jit(solution)/shard_map/ppermute | solution.py:16
  196.8 29.2 %collective-permute-start = (bf16[2,1,640,192]{2,3,1,0:T(8,128)(2,1)}, bf16[2,1,640,192]{2,3,1,0:T(8,128)(2,1)S(1)}, u32[]{:S(2)}, u32[]{:S(2)}) collective-permute-start(bf16[2,1,640,192]{2,3,1,0:T(8,128)(2,1)} %get-tuple-element.11), channel_id=1, source_target_pairs={{0,1},{1,2},{2,3},{3,4},{4,5},{5,6},{6,7},{7,8},{8,9},{9,10},{10,1... | collective-permute-start | bytes 1474568 | tf_op jit(solution)/shard_map/ppermute | solution.py:24
  198.7 27.2 %collective-permute-start.1 = (bf16[2,1,640,192]{2,3,1,0:T(8,128)(2,1)}, bf16[2,1,640,192]{2,3,1,0:T(8,128)(2,1)}, u32[]{:S(2)}, u32[]{:S(2)}) collective-permute-start(bf16[2,1,640,192]{2,3,1,0:T(8,128)(2,1)} %get-tuple-element.12), channel_id=1, source_target_pairs={{1,0},{2,1},{3,2},{4,3},{5,4},{6,5},{7,6},{8,7},{9,8},{10,9},{11,1... | collective-permute-start | bytes 1474568 | tf_op jit(solution)/shard_map/ppermute | solution.py:27
  225.9 69.6 %copy-start.2 = (bf16[2,8,640,192]{2,3,1,0:T(8,128)(2,1)S(1)}, bf16[2,8,640,192]{2,3,1,0:T(8,128)(2,1)}, u32[]{:S(2)}) copy-start(bf16[2,8,640,192]{2,3,1,0:T(8,128)(2,1)} %copy.130) | copy-start | bytes 11796484
  329.6 15.5 %copy-start.5 = (bf16[3,3,3,192,96]{4,3,2,1,0:T(8,128)(2,1)S(1)}, bf16[3,3,3,192,96]{4,3,2,1,0:T(8,128)(2,1)}, u32[]{:S(2)}) copy-start(bf16[3,3,3,192,96]{4,3,2,1,0:T(8,128)(2,1)} %reshape.48) | copy-start | bytes 2985988
  329.6 15.5 %copy-start.12 = (pred[8,81]{0,1:T(8,128)(4,1)S(1)}, pred[8,81]{0,1:T(8,128)(4,1)}, u32[]{:S(2)}) copy-start(pred[8,81]{0,1:T(8,128)(4,1)} %constant.39) | copy-start | bytes 1948
  340.3 4.7 %copy-start.3 = (bf16[4,10,1,8,81,192]{5,3,4,1,0,2:T(8,128)(2,1)}, bf16[4,10,1,8,81,192]{5,3,4,1,0,2:T(8,128)(2,1)S(1)}, u32[]{:S(2)}) copy-start(bf16[4,10,1,8,81,192]{5,3,4,1,0,2:T(8,128)(2,1)S(1)} %copy.133) | copy-start | bytes 29859844
  387.1 5.9 %copy-start.6 = (bf16[192,96]{1,0:T(8,128)(2,1)S(1)}, bf16[192,96]{1,0:T(8,128)(2,1)}, u32[]{:S(2)}) copy-start(bf16[192,96]{1,0:T(8,128)(2,1)} %param.18) | copy-start | bytes 110596
  387.1 5.9 %copy-start.9 = (f32[96]{0:T(128)S(1)}, f32[96]{0:T(128)}, u32[]{:S(2)}) copy-start(f32[96]{0:T(128)} %param.21) | copy-start | bytes 1156
  393.0 13.0 %copy-start.1 = (bf16[3,3,384,192]{2,3,1,0:T(8,128)(2,1)S(1)}, bf16[3,3,384,192]{2,3,1,0:T(8,128)(2,1)}, u32[]{:S(2)}) copy-start(bf16[3,3,384,192]{2,3,1,0:T(8,128)(2,1)} %param.16) | copy-start | bytes 3981316
where the time goes:
time: 414 us; the launch traced here: 406 us
  local copies, waits for them, and re-layouts  144 us (35%)
  waiting for transfers between devices  87.8 us (21%)
  matrix products  71.8 us (17%)
  starting transfers between devices  48.1 us (12%)
  other arithmetic  47.8 us (12%)
  blocking collectives  6.37 us (2%)
    ppermute x2, waiting for transfers between devices, passed_along(): return lax.ppermute(value, axis, pairs)  69 us
    conv_general_dilated x2, matrix products, conv_time(): lax.conv_general_dilated(field[None], kernel, (1, 1, 1), [(0, 0), (0, 0),...  42.5 us
    unnamed x34, local copies, waits for them, and re-layouts  39.7 us
    ppermute x4, starting transfers between devices, padded(): lax.ppermute(lax.slice_in_dim(block, 0, width, axis=dim), axis, backward)  37.6 us
    conv_general_dilated x1, matrix products, conv_plane(): lax.conv_general_dilated(field, kernel, (1, 1), [(0, 0), (col_pad, col_pa...  24.9 us
    concatenate x2, other arithmetic, padded(): block = jnp.concatenate([low, block, high], axis=dim)  22.1 us
    conv_general_dilated x9, local copies, waits for them, and re-layouts, conv_time(): lax.conv_general_dilated(field[None], kernel, (1, 1, 1), [(0, 0), (0, 0),...  20.6 us
    ppermute x4, waiting for transfers between devices, padded(): lax.ppermute(lax.slice_in_dim(block, block.shape[dim] - width, None, axis...  15.3 us
  transfers between devices with their start and end apart: 10, of which 6 were waited for; matrix products, arithmetic and copies ran while one was open for 7% of the time, Pallas kernels for 0%

commit v1 on v0

v1 whole, which is shorter than its diff:
```python
import functools

import jax
import jax.numpy as jnp
from jax import lax
from jax.experimental import pallas as pl
from jax.experimental.pallas import tpu as pltpu
from jax.sharding import PartitionSpec as P

C0 = 16
C1 = 384
C2 = 192
C3 = 96
FRAMES = 4
PATCH_COLS = 80
HALO = 16
TOK = PATCH_COLS + 2 * HALO
WIDE = 96
FCOLS = 320
BF = jnp.bfloat16
F32 = jnp.float32
MESH = pl.DeviceIdType.MESH


def silu_half(half):
    return half + half * jnp.tanh(half)


def kernel(
    tokens,
    cache_lat,
    cache_feat,
    w1_hbm,
    w2_hbm,
    w3_hbm,
    b1,
    b2,
    b3,
    g1,
    g2,
    out,
    tok,
    win,
    y1,
    a_r0,
    a_r1p,
    a_r1c,
    y2e,
    y2o,
    fe,
    fo,
    fe1,
    ue,
    uo,
    cf,
    cs,
    acc,
    ostage,
    w1,
    w2,
    w3,
    send_sem,
    recv_sem,
    local_sem,
):
    ta = lax.axis_index("ta")
    ha = lax.axis_index("ha")
    n_ha = lax.axis_size("ha")
    up = lax.rem(ha + n_ha - 1, n_ha)
    down = lax.rem(ha + 1, n_ha)
    other = 1 - ta
    top = ha == 0
    bottom = ha == n_ha - 1
    left = ta == 0

    lat_src = pl.multiple_of(ta * 64, 16)
    lat_dst = pl.multiple_of(HALO - ta * HALO, 16)
    feat_src = pl.multiple_of(ta * 304, 16)
    feat_dst = pl.multiple_of(HALO - ta * HALO, 16)
    edge_src = pl.multiple_of((1 - ta) * 64, 16)
    edge_dst = pl.multiple_of(ta * 96, 16)
    local = [
        pltpu.make_async_copy(
            tokens, tok.at[2:6, 1:3, HALO : HALO + PATCH_COLS], local_sem.at[0]
        ),
        pltpu.make_async_copy(
            cache_lat.at[:, :, pl.ds(lat_src, 96)],
            tok.at[0:2, 1:3, pl.ds(lat_dst, 96)],
            local_sem.at[1],
        ),
        pltpu.make_async_copy(w1_hbm, w1, local_sem.at[2]),
        pltpu.make_async_copy(w2_hbm, w2, local_sem.at[3]),
        pltpu.make_async_copy(
            cache_feat.at[:, :, pl.ds(feat_src, 336)],
            cf.at[:, 1:9, pl.ds(feat_dst, 336)],
            local_sem.at[4],
        ),
        pltpu.make_async_copy(w3_hbm, w3, local_sem.at[5]),
    ]
    for copy in local:
        copy.start()

    barrier = pltpu.get_barrier_semaphore()
    partners = [(ta, up), (ta, down), (other, ha), (other, up), (other, down)]
    for partner in partners:
        pl.semaphore_signal(barrier, inc=1, device_id=partner, device_id_type=MESH)
    pl.semaphore_wait(barrier, len(partners))

    def remote(slot, src, dst, to):
        return pltpu.make_async_remote_copy(
            src_ref=src,
            dst_ref=dst,
            send_sem=send_sem.at[slot],
            recv_sem=recv_sem.at[slot],
            device_id=to,
            device_id_type=MESH,
        )

    own = slice(HALO, HALO + PATCH_COLS)
    early = [
        remote(0, tokens.at[:, 0], tok.at[2:6, 3, own], (ta, up)),
        remote(1, tokens.at[:, 1], tok.at[2:6, 0, own], (ta, down)),
        remote(
            2,
            tokens.at[:, :, pl.ds(edge_src, HALO)],
            tok.at[2:6, 1:3, pl.ds(edge_dst, HALO)],
            (other, ha),
        ),
        remote(
            3,
            tokens.at[:, 0, pl.ds(edge_src, HALO)],
            tok.at[2:6, 3, pl.ds(edge_dst, HALO)],
            (other, up),
        ),
        remote(
            4,
            tokens.at[:, 1, pl.ds(edge_src, HALO)],
            tok.at[2:6, 0, pl.ds(edge_dst, HALO)],
            (other, down),
        ),
        remote(
            5,
            cache_lat.at[:, 0, pl.ds(lat_src, 96)],
            tok.at[0:2, 3, pl.ds(lat_dst, 96)],
            (ta, up),
        ),
        remote(
            6,
            cache_lat.at[:, 1, pl.ds(lat_src, 96)],
            tok.at[0:2, 0, pl.ds(lat_dst, 96)],
            (ta, down),
        ),
    ]
    later = [
        remote(
            7,
            cache_feat.at[:, 0, pl.ds(feat_src, 336)],
            cf.at[:, 9, pl.ds(feat_dst, 336)],
            (ta, up),
        ),
        remote(
            8,
            cache_feat.at[:, 7, pl.ds(feat_src, 336)],
            cf.at[:, 0, pl.ds(feat_dst, 336)],
            (ta, down),
        ),
    ]
    for copy in early + later:
        copy.start()

    @pl.when(left)
    def _():
        tok[:, :, 0:HALO] = jnp.zeros((6, 4, HALO, 4 * C0), BF)
        cf[:, :, 0:HALO] = jnp.zeros((2, 10, HALO, C2), BF)

    @pl.when(jnp.logical_not(left))
    def _():
        tok[:, :, HALO + PATCH_COLS :] = jnp.zeros((6, 4, HALO, 4 * C0), BF)
        cf[:, :, HALO + FCOLS :] = jnp.zeros((2, 10, HALO, C2), BF)

    for copy in early:
        copy.wait()
    local[0].wait()
    local[1].wait()

    @pl.when(top)
    def _():
        tok[:, 0] = jnp.zeros((6, TOK, 4 * C0), BF)

    @pl.when(bottom)
    def _():
        tok[:, 3] = jnp.zeros((6, TOK, 4 * C0), BF)

    lane64 = lax.broadcasted_iota(jnp.int32, (TOK, 4 * C0), 1)
    second_row = lane64 >= 2 * C0
    second_col = (lane64 // C0) % 2 == 1

    def windows(t, carry):
        rows = [tok[t, u].astype(F32) for u in range(4)]
        for u in range(4):
            above = rows[max(u - 1, 0)]
            below = rows[min(u + 1, 3)]
            here = rows[u]
            vert = jnp.where(second_row, above, below)
            horiz = jnp.where(second_col, pltpu.roll(here, 1, 0), pltpu.roll(here, TOK - 1, 0))
            diag = jnp.where(second_col, pltpu.roll(vert, 1, 0), pltpu.roll(vert, TOK - 1, 0))
            full = jnp.concatenate([here, vert, horiz, diag], axis=1)
            win[t, u] = pltpu.roll(full, 1, 0)[HALO : HALO + WIDE].astype(BF)
        return carry

    lax.fori_loop(0, 6, windows, 0)
    local[2].wait()

    def first(row, carry):
        u = (row + 1) // 2
        q = (row + 1) % 2
        lhs = jnp.concatenate(
            [win[dt : dt + 4, u].reshape(4 * WIDE, 256) for dt in range(3)], axis=1
        )
        y1[...] = jnp.dot(lhs, w1[q], preferred_element_type=F32)

        def finish(f, inner):
            base = pl.multiple_of(f * WIDE, WIDE)
            acts = []
            for r in range(2):
                v = y1[pl.ds(base, WIDE), r * C1 : (r + 1) * C1] + b1[...]
                scale = lax.rsqrt(jnp.mean(v * v, axis=1, keepdims=True) + 1e-06)
                acts.append(silu_half(v * scale * (0.5 * g1[...])))
            a_r0[f, row] = pltpu.roll(acts[0], WIDE - 1, 0).astype(BF)
            a_r1p[f, row] = acts[1].astype(BF)
            a_r1c[f, row] = pltpu.roll(acts[1], WIDE - 1, 0)[:PATCH_COLS].astype(BF)
            return inner

        lax.fori_loop(0, 4, finish, 0)
        return carry

    lax.fori_loop(0, 6, first, 0)

    @pl.when(top)
    def _():
        a_r0[:, 0] = jnp.zeros((4, WIDE, C1), BF)
        a_r1p[:, 0] = jnp.zeros((4, WIDE, C1), BF)
        a_r1c[:, 0] = jnp.zeros((4, PATCH_COLS, C1), BF)

    @pl.when(bottom)
    def _():
        a_r0[:, 5] = jnp.zeros((4, WIDE, C1), BF)
        a_r1p[:, 5] = jnp.zeros((4, WIDE, C1), BF)
        a_r1c[:, 5] = jnp.zeros((4, PATCH_COLS, C1), BF)

    sub16 = lax.broadcasted_iota(jnp.int32, (16, 2 * C2), 0)
    lane16 = lax.broadcasted_iota(jnp.int32, (16, 2 * C2), 1)

    @pl.when(left)
    def _():
        for f in range(4):
            for row in range(6):
                kept = a_r1p[f, row, 0:16].astype(F32)
                a_r1p[f, row, 0:16] = jnp.where(sub16 == 0, 0.0, kept).astype(BF)

    @pl.when(jnp.logical_not(left))
    def _():
        a_r0[:, :, PATCH_COLS:] = jnp.zeros((4, 6, WIDE - PATCH_COLS, C1), BF)

    local[4].wait()
    for copy in later:
        copy.wait()

    @pl.when(top)
    def _():
        cf[:, 0] = jnp.zeros((2, FCOLS + 2 * HALO, C2), BF)

    @pl.when(bottom)
    def _():
        cf[:, 9] = jnp.zeros((2, FCOLS + 2 * HALO, C2), BF)

    def cached(n, carry):
        t = n // 10
        row = n % 10
        wide = cf[t, row].astype(F32)
        cs[0] = wide[:, 0:128]
        cs[1, :, 0:64] = wide[:, 128:192]

        def columns(start):
            part = pl.ds(start, PATCH_COLS, stride=4)
            return jnp.concatenate([cs[0, part, :], cs[1, part, :][:, :64]], axis=1)

        for ref, start in ((fe, 15), (fo, 17), (fe1, 19)):
            pair = jnp.concatenate([columns(start), columns(start + 1)], axis=1)
            ref[t, row] = pair.astype(BF)
        return carry

    lax.fori_loop(0, 20, cached, 0)
    local[3].wait()

    low_half = lax.broadcasted_iota(jnp.int32, (1, 128), 1) < 64

    def norm_pair(v):
        v0, v1, v2 = v[:, 0:128], v[:, 128:256], v[:, 256:384]
        sq1 = v1 * v1
        sum_a = jnp.sum(v0 * v0 + jnp.where(low_half, sq1, 0.0), axis=1, keepdims=True)
        sum_b = jnp.sum(v2 * v2 + jnp.where(low_half, 0.0, sq1), axis=1, keepdims=True)
        scale_a = lax.rsqrt(sum_a * (1.0 / C2) + 1e-06)
        scale_b = lax.rsqrt(sum_b * (1.0 / C2) + 1e-06)
        scaled = jnp.concatenate(
            [v0 * scale_a, v1 * jnp.where(low_half, scale_a, scale_b), v2 * scale_b], axis=1
        )
        return silu_half(scaled * (0.5 * g2[...]))

    first_col = lax.broadcasted_iota(jnp.int32, (1, 2 * C2), 1) < C2

    def second(f):
        lhs = jnp.concatenate(
            [a_r1p[f, 0:5], a_r0[f, 0:5], a_r1p[f, 1:6], a_r0[f, 1:6]], axis=2
        ).reshape(5 * WIDE, 4 * C1)
        y2e[...] = jnp.dot(lhs, w2[...], preferred_element_type=F32)
        lhs = jnp.concatenate(
            [a_r0[f, 0:5, :PATCH_COLS], a_r1c[f, 0:5], a_r0[f, 1:6, :PATCH_COLS], a_r1c[f, 1:6]],
            axis=2,
        ).reshape(5 * PATCH_COLS, 4 * C1)
        y2o[...] = jnp.dot(lhs, w2[...], preferred_element_type=F32)

        def finish(i, carry):
            for par in range(2):
                row = 2 * i + par
                cols = slice(par * 384, (par + 1) * 384)
                ve = y2e[pl.ds(pl.multiple_of(i * WIDE, WIDE), WIDE), cols] + b2[...]
                vo = y2o[pl.ds(pl.multiple_of(i * PATCH_COLS, 16), PATCH_COLS), cols] + b2[...]
                act = norm_pair(ve)
                fe[f + 2, row] = act[:PATCH_COLS].astype(BF)
                fe1[f + 2, row] = pltpu.roll(act, WIDE - 1, 0)[:PATCH_COLS].astype(BF)
                fo[f + 2, row] = norm_pair(vo).astype(BF)
                ve1 = pltpu.roll(ve, WIDE - 1, 0)[:PATCH_COLS]
                ue[f, row] = jnp.where(first_col, vo, ve[:PATCH_COLS]).astype(BF)
                uo[f, row] = jnp.where(first_col, ve1, vo).astype(BF)
            return carry

        lax.fori_loop(0, 5, finish, 0)

        @pl.when(top)
        def _():
            for ref in (fe, fo, fe1):
                ref[f + 2, 0] = jnp.zeros((PATCH_COLS, 2 * C2), BF)

        @pl.when(bottom)
        def _():
            for ref in (fe, fo, fe1):
                ref[f + 2, 9] = jnp.zeros((PATCH_COLS, 2 * C2), BF)

        @pl.when(left)
        def _():
            for row in range(10):
                kept = fe[f + 2, row, 0:16].astype(F32)
                gone = jnp.logical_and(sub16 == 0, lane16 < C2)
                fe[f + 2, row, 0:16] = jnp.where(gone, 0.0, kept).astype(BF)

        @pl.when(jnp.logical_not(left))
        def _():
            for row in range(10):
                kept = fe1[f + 2, row, 64:80].astype(F32)
                gone = jnp.logical_and(sub16 == 15, lane16 >= C2)
                fe1[f + 2, row, 64:80] = jnp.where(gone, 0.0, kept).astype(BF)

    def third(f):
        def rows4(n, carry):
            y = n * 4
            blocks = []
            for dt in range(3):
                for dr in range(3):
                    part = pl.ds(y + dr, 4)
                    e, o, e1 = fe[f + dt, part], fo[f + dt, part], fe1[f + dt, part]
                    blocks.append(
                        jnp.concatenate(
                            [
                                jnp.concatenate([e, o], axis=2),
                                jnp.concatenate([o, e1], axis=2),
                            ],
                            axis=0,
                        ).reshape(8 * PATCH_COLS, 768)
                    )
            mine = pl.ds(y + 1, 4)
            blocks.append(
                jnp.concatenate([ue[f, mine], uo[f, mine]], axis=0).reshape(8 * PATCH_COLS, 384)
            )
            res = jnp.dot(
                jnp.concatenate(blocks, axis=1), w3[...], preferred_element_type=F32
            )
            half = 4 * PATCH_COLS
            both = jnp.concatenate([res[:half], res[half:]], axis=1)
            for piece in range(3):
                acc[piece, pl.ds(pl.multiple_of(y * PATCH_COLS, 16), half), :] = both[
                    :, piece * 128 : (piece + 1) * 128
                ]
            return carry

        lax.fori_loop(0, 2, rows4, 0)

        def turn(s, carry):
            part = pl.ds(s, 8, stride=PATCH_COLS)
            x = jnp.concatenate([acc[piece, part, :] for piece in range(3)], axis=1) + b3[...]
            ostage[f, :, pl.ds(pl.multiple_of(s * 384, 128), 384)] = x.astype(BF)
            return carry

        lax.fori_loop(0, PATCH_COLS, turn, 0)

    for f in range(3):
        second(f)
    local[5].wait()

    half_lanes = PATCH_COLS * 384
    lanes = pl.ds(pl.multiple_of(ta * half_lanes, 128), half_lanes)

    def sent(k):
        f = 2 * other + k
        return remote(9 + k, ostage.at[f], out.at[k, :, lanes], (other, ha))

    def kept(k):
        f = 2 * ta + k
        return pltpu.make_async_copy(ostage.at[f], out.at[k, :, lanes], local_sem.at[6 + k])

    third(2 * other)
    sent(0).start()
    second(3)
    third(2 * other + 1)
    sent(1).start()
    third(2 * ta)
    kept(0).start()
    third(2 * ta + 1)
    kept(1).start()
    for k in range(2):
        kept(k).wait()
    for k in range(2):
        sent(k).wait()


def first_weight(weight_in):
    outs = []
    for q in range(2):
        cols = []
        for r in range(2):
            w = jnp.pad(weight_in, ((0, 0), (q, 1 - q), (r, 1 - r), (0, 0), (0, 0)))
            w = jnp.roll(w, (-1, -1), (1, 2)).reshape(3, 2, 2, 2, 2, C0, C1)
            cols.append(w.transpose(0, 3, 1, 2, 4, 5, 6).reshape(768, C1))
        outs.append(jnp.concatenate(cols, axis=1))
    return jnp.stack(outs)


def second_weight(weight_up):
    w = weight_up.astype(F32)

    def pick(arr, axis, k, par):
        s = functools.partial(lax.index_in_dim, arr, axis=axis, keepdims=False)
        return {
            (0, 0): lambda: s(0) + s(1),
            (1, 0): lambda: s(2),
            (0, 1): lambda: s(0),
            (1, 1): lambda: s(1) + s(2),
        }[(k, par)]()

    rows = []
    for kr in range(2):
        for kc in range(2):
            rows.append(
                jnp.concatenate(
                    [pick(pick(w, 0, kr, pr), 0, kc, pc) for pr in range(2) for pc in range(2)],
                    axis=1,
                )
            )
    return jnp.concatenate(rows, axis=0).astype(BF)


def third_weight(weight_out, weight_skip):
    w = weight_out.reshape(9, 3 * C2, C3)
    z = jnp.zeros((9, C2, C3), BF)
    main = jnp.concatenate(
        [jnp.concatenate([w, z], axis=1), jnp.concatenate([z, w], axis=1)], axis=2
    ).reshape(9 * 768, 2 * C3)
    zs = jnp.zeros((C2, C3), BF)
    skip = jnp.concatenate(
        [jnp.concatenate([zs, weight_skip], axis=1), jnp.concatenate([weight_skip, zs], axis=1)],
        axis=0,
    )
    return jnp.concatenate([main, skip], axis=0)


def shards(
    tokens,
    cache_latent,
    cache_feature,
    weight_in,
    weight_up,
    weight_out,
    weight_skip,
    bias_in,
    bias_up,
    bias_out,
    gain_in,
    gain_up,
):
    tok = tokens.reshape(4, 2, PATCH_COLS, 4 * C0)
    lat = (
        cache_latent.reshape(2, 2, 2, 160, 2, C0)
        .transpose(0, 1, 3, 2, 4, 5)
        .reshape(2, 2, 160, 4 * C0)
    )
    any_spec = pl.BlockSpec(memory_space=pl.ANY)
    vmem = pl.BlockSpec(memory_space=pltpu.VMEM)
    scratch = [
        pltpu.VMEM((6, 4, TOK, 4 * C0), BF),
        pltpu.VMEM((6, 4, WIDE, 256), BF),
        pltpu.VMEM((4 * WIDE, 2 * C1), F32),
        pltpu.VMEM((4, 6, WIDE, C1), BF),
        pltpu.VMEM((4, 6, WIDE, C1), BF),
        pltpu.VMEM((4, 6, PATCH_COLS, C1), BF),
        pltpu.VMEM((5 * WIDE, 4 * C2), F32),
        pltpu.VMEM((5 * PATCH_COLS, 4 * C2), F32),
        pltpu.VMEM((6, 10, PATCH_COLS, 2 * C2), BF),
        pltpu.VMEM((6, 10, PATCH_COLS, 2 * C2), BF),
        pltpu.VMEM((6, 10, PATCH_COLS, 2 * C2), BF),
        pltpu.VMEM((4, 10, PATCH_COLS, 2 * C2), BF),
        pltpu.VMEM((4, 10, PATCH_COLS, 2 * C2), BF),
        pltpu.VMEM((2, 10, FCOLS + 2 * HALO, C2), BF),
        pltpu.VMEM((2, FCOLS + 2 * HALO, 128), F32),
        pltpu.VMEM((3, 8 * PATCH_COLS, 128), F32),
        pltpu.VMEM((4, 8, PATCH_COLS * 384), BF),
        pltpu.VMEM((2, 768, 2 * C1), BF),
        pltpu.VMEM((4 * C1, 4 * C2), BF),
        pltpu.VMEM((9 * 768 + 384, 2 * C3), BF),
        pltpu.SemaphoreType.DMA((11,)),
        pltpu.SemaphoreType.DMA((11,)),
        pltpu.SemaphoreType.DMA((8,)),
    ]
    return pl.pallas_call(
        kernel,
        out_shape=jax.ShapeDtypeStruct((2, 8, 640 * C3), BF),
        in_specs=[any_spec] * 6 + [vmem] * 5,
        out_specs=any_spec,
        scratch_shapes=scratch,
        compiler_params=pltpu.CompilerParams(
            collective_id=0, has_side_effects=True, vmem_limit_bytes=60 * 1024 * 1024
        ),
        cost_estimate=pl.CostEstimate(
            flops=28_000_000_000, bytes_accessed=16_000_000, transcendentals=5_000_000
        ),
    )(
        tok,
        lat,
        cache_feature,
        first_weight(weight_in),
        second_weight(weight_up),
        third_weight(weight_out, weight_skip),
        bias_in.reshape(1, C1),
        jnp.tile(bias_up, 2).reshape(1, 2 * C2),
        jnp.tile(bias_out, 4).reshape(1, 4 * C3),
        gain_in.reshape(1, C1),
        jnp.tile(gain_up, 2).reshape(1, 2 * C2),
    )


def solution(mesh):
    placed = (
        P(None, "ha", "ta"),
        P(None, "ha", None),
        P(None, "ha", None, None),
        P(),
        P(),
        P(),
        P(),
        P(),
        P(),
        P(),
        P(),
        P(),
    )
    return jax.shard_map(
        shards, mesh=mesh, in_specs=placed, out_specs=P("ta", "ha", None), check_vma=False
    )
```

time: 414 us -> 140 us (0.34)
  the two profiles are of different devices: /device:TPU:24 before, /device:TPU:0 now
where the time goes in v1:
time: 140 us; the launch traced here: 139 us
  Pallas kernels  67.7 us (48%)
  other arithmetic  44.2 us (32%)
  local copies, waits for them, and re-layouts  26.9 us (19%)
    pallas_call x1, Pallas kernels, shards(): pl.pallas_call(kernel, out_shape=jax.ShapeDtypeStruct((2, 8, 640 * C3), B...  67.7 us
    concatenate x1, other arithmetic, second_weight(): return jnp.concatenate(rows, axis=0).astype(BF)  26.7 us
    unnamed x9, local copies, waits for them, and re-layouts  12.9 us
    concatenate x1, other arithmetic, third_weight(): return jnp.concatenate([main, skip], axis=0)  12 us

profile of v1, /device:TPU:0, one launch (start us, length us, event | category | flops | bytes accessed | tf_op | source)
XLA Modules:
  0.0 139.0 jit_solution(11526732378819029101)
XLA Ops:
  0.0 0.0 copy-start
  0.0 1.4 reshape.87.b1
  1.4 1.3 reshape.88.g1
  2.7 0.7 tile.6
  3.3 0.7 reshape_tile.9.b2
  4.0 0.7 tile.7
  4.7 0.7 reshape_tile.10.b3
  5.3 0.7 tile.8
  6.0 0.7 reshape_tile.11.g2
  6.7 1.7 %reshape.74.tokens = bf16[4,2,80,64]{3,2,1,0:T(8,128)(2,1)} reshape(bf16[4,2,5120]{2,1,0:T(2,128)(2,1)} %param.12) | data formatting | bytes 163840 | tf_op jit(solution)/shard_map/reshape | solution.py:500
  8.4 1.0 pad_slice_fusion.2
  9.4 1.4 reshape.75
  10.8 0.4 copy.20
  11.2 0.8 copy.26.cache_lat
  12.0 0.0 copy-done
  12.0 1.2 reshape.85
  13.2 2.5 %copy.25 = bf16[3,3,384,192]{3,2,1,0:T(8,128)(2,1)S(1)} copy(bf16[3,3,384,192]{2,3,1,0:T(8,128)(2,1)} %param.16) | data formatting | bytes 2654208 | tf_op args[4]
  15.7 0.3 convert_element_type.12
  16.1 0.1 fusion.13
  16.2 0.2 fusion.21
  16.4 0.3 slice_add_fusion.1
  16.7 0.2 fusion.20
  16.9 0.0 copy-start.1
  16.9 0.1 fusion.12
  17.0 26.7 %maximum_maximum_fusion.w2_hbm = bf16[1536,768]{1,0:T(8,128)(2,1)} fusion(bf16[384,192]{1,0:T(8,128)(2,1)S(1)} %get-tuple-element.37, bf16[384,192]{1,0:T(8,128)(2,1)S(1)} %get-tuple-element.35, bf16[384,192]{1,0:T(8,128)(2,1)S(1)} %get-tuple-element.8, bf16[384,192]{1,0:T(8,128)(2,1)S(1)} %get-tuple-element.11, bf16[384,192]{1,0:T(8,128)(2,1)S(1)} %get-tuple-element.36, ...), kind=kLoop, calls=%fused_computation.14 | loop fusion | flops 37748736 | bytes 4718592 | tf_op jit(solution)/shard_map/concatenate | solution.py:469
  43.7 0.0 copy-done.1
  43.7 0.2 pad_slice_fusion.3
  43.9 0.1 pad_slice_fusion.5
  44.0 0.1 pad_maximum_fusion.4
  44.1 0.1 copy.24
  44.2 0.1 pad_maximum_fusion.3
  44.3 0.1 copy.23
  44.3 0.1 maximum_bitcast_fusion.1
  44.4 0.1 fusion.11
  44.5 0.1 fusion.10
  44.6 0.1 fusion.8
  44.7 0.1 copy.22
  44.8 0.1 copy.21
  44.9 0.1 maximum_bitcast_fusion
  45.0 1.6 %pad_maximum_fusion.w1_hbm = bf16[2,768,768]{2,1,0:T(8,128)(2,1)} fusion(bf16[1,768,768]{2,1,0:T(8,128)(2,1)S(1)} %maximum_bitcast_fusion.1, bf16[1,768,768]{2,1,0:T(8,128)(2,1)S(1)} %maximum_bitcast_fusion), kind=kLoop, calls=%fused_computation.13 | loop fusion | flops 1179648 | bytes 4718592 | tf_op jit(solution)/shard_map/stack | solution.py:445
  46.6 0.0 copy-start.2
  46.6 2.2 %fusion.7 = bf16[9,768,192]{2,1,0:T(8,128)(2,1)S(1)} fusion(bf16[9,576,96]{2,1,0:T(8,128)(2,1)S(1)} %reshape.85), kind=kLoop, calls=%fused_computation.12 | loop fusion | flops 10616832 | bytes 3649536 | tf_op jit(solution)/shard_map/concatenate | solution.py:475
  48.9 0.0 copy-done.2
  48.9 12.0 %fusion.6.w3_hbm = bf16[7296,192]{1,0:T(8,128)(2,1)} fusion(bf16[192,96]{1,0:T(8,128)(2,1)S(1)} %copy-done.2, bf16[6912,192]{1,0:T(8,128)(2,1)S(1)} %bitcast.55), kind=kLoop, calls=%fused_computation.11 | loop fusion | flops 16809984 | bytes 5492736 | tf_op jit(solution)/shard_map/concatenate | solution.py:483
  60.9 7.4 %copy.27.cache_feat = bf16[2,8,640,192]{3,2,1,0:T(8,128)(2,1)} copy(bf16[2,8,640,192]{2,3,1,0:T(8,128)(2,1)} %param.14) | data formatting | bytes 7864320 | tf_op args[2]
  68.3 67.7 %shard_map.118 = bf16[2,8,61440]{2,1,0:T(8,128)(2,1)} custom-call(bf16[4,2,80,64]{3,2,1,0:T(8,128)(2,1)} %reshape.74.tokens, bf16[2,2,160,64]{3,2,1,0:T(8,128)(2,1)} %copy.26.cache_lat, bf16[2,8,640,192]{3,2,1,0:T(8,128)(2,1)} %copy.27.cache_feat, bf16[2,768,768]{2,1,0:T(8,128)(2,1)} %pad_maximum_fusion.w1_hbm, ...), custom_call_target="tpu_custom_call" | custom-call | flops 28000000000 | bytes 16000000 | tf_op jit(solution)/shard_map/pallas_call | solution.py:533
  136.0 2.9 %copy.29 = bf16[2,8,61440]{2,1,0:T(8,128)(2,1)} copy(bf16[2,8,61440]{2,1,0:T(8,128)(2,1)} %shard_map.118) | data formatting | bytes 3932160
  (1 shorter events, 0.0 us)
Async XLA Ops:
  0.0 12.0 %copy-start = (bf16[3,3,3,18432]{3,2,1,0:T(4,128)(2,1)S(1)}, bf16[3,3,3,18432]{3,2,1,0:T(4,128)(2,1)}, u32[]{:S(2)}) copy-start(bf16[3,3,3,18432]{3,2,1,0:T(4,128)(2,1)} %param.17) | copy-start | bytes 2985988
  16.9 26.8 %copy-start.1 = (bf16[3,3,3,16,384]{4,3,2,1,0:T(8,128)(2,1)S(1)}, bf16[3,3,3,16,384]{4,3,2,1,0:T(8,128)(2,1)}, u32[]{:S(2)}) copy-start(bf16[3,3,3,16,384]{4,3,2,1,0:T(8,128)(2,1)} %param.15) | copy-start | bytes 995332
  46.6 2.3 %copy-start.2 = (bf16[192,96]{1,0:T(8,128)(2,1)S(1)}, bf16[192,96]{1,0:T(8,128)(2,1)}, u32[]{:S(2)}) copy-start(bf16[192,96]{1,0:T(8,128)(2,1)} %param.18) | copy-start | bytes 110596

commit v2 on v1

v2 whole, which is shorter than its diff:
```python
import functools

import jax
import jax.numpy as jnp
from jax import lax
from jax.experimental import pallas as pl
from jax.experimental.pallas import tpu as pltpu
from jax.sharding import PartitionSpec as P

C0 = 16
C1 = 384
C2 = 192
C3 = 96
FRAMES = 4
PATCH_COLS = 80
HALO = 16
TOK = PATCH_COLS + 2 * HALO
WIDE = 96
FEAT = 384
BF = jnp.bfloat16
F32 = jnp.float32
MESH = pl.DeviceIdType.MESH


def silu_half(half):
    return half + half * jnp.tanh(half)


def kernel(
    tokens,
    cache_lat,
    cache_feat,
    w_in_hbm,
    w_up_hbm,
    w_out_hbm,
    w_skip,
    b1,
    b2,
    b3,
    g1,
    g2,
    out,
    tok,
    lat,
    win,
    y1a,
    y1b,
    a_r0,
    a_r1p,
    a_r1c,
    y2e,
    y2o,
    fe,
    fo,
    fe1,
    ue,
    uo,
    cf,
    cf_edge,
    pick,
    acc_a,
    acc_b,
    ostage,
    w_in,
    w_up,
    w_out,
    w1,
    w2,
    w3,
    send_sem,
    recv_sem,
    local_sem,
):
    ta = lax.axis_index("ta")
    ha = lax.axis_index("ha")
    n_ha = lax.axis_size("ha")
    up = jnp.maximum(ha - 1, 0)
    down = jnp.minimum(ha + 1, n_ha - 1)
    other = 1 - ta
    top = ha == 0
    bottom = ha == n_ha - 1
    left = ta == 0

    lat_src = pl.multiple_of(ta * 64, 16)
    lat_dst = pl.multiple_of(HALO - ta * HALO, 16)
    feat = pl.ds(pl.multiple_of(ta * 256, 128), 384)
    edge_src = pl.multiple_of((1 - ta) * 64, 16)
    edge_dst = pl.multiple_of(ta * 96, 16)
    local = [
        pltpu.make_async_copy(
            tokens, tok.at[:, 1:3, HALO : HALO + PATCH_COLS], local_sem.at[0]
        ),
        pltpu.make_async_copy(
            cache_lat.at[:, :, pl.ds(lat_src, 96)],
            lat.at[:, 2:6, pl.ds(lat_dst, 96)],
            local_sem.at[1],
        ),
        pltpu.make_async_copy(w_in_hbm, w_in, local_sem.at[2]),
        pltpu.make_async_copy(w_up_hbm, w_up, local_sem.at[3]),
        pltpu.make_async_copy(cache_feat.at[:, :, :, feat], cf, local_sem.at[4]),
        pltpu.make_async_copy(w_out_hbm, w_out, local_sem.at[5]),
    ]
    for copy in local:
        copy.start()

    barrier = pltpu.get_barrier_semaphore()

    def hello(partner):
        pl.semaphore_signal(barrier, inc=1, device_id=partner, device_id_type=MESH)

    hello((other, ha))

    @pl.when(jnp.logical_not(top))
    def _():
        hello((ta, up))
        hello((other, up))

    @pl.when(jnp.logical_not(bottom))
    def _():
        hello((ta, down))
        hello((other, down))

    def remote(slot, src, dst, to):
        return pltpu.make_async_remote_copy(
            src_ref=src,
            dst_ref=dst,
            send_sem=send_sem.at[slot],
            recv_sem=recv_sem.at[slot],
            device_id=to,
            device_id_type=MESH,
        )

    own = slice(HALO, HALO + PATCH_COLS)
    to_up = [
        remote(0, tokens.at[:, 0], tok.at[:, 3, own], (ta, up)),
        remote(
            1,
            tokens.at[:, 0, pl.ds(edge_src, HALO)],
            tok.at[:, 3, pl.ds(edge_dst, HALO)],
            (other, up),
        ),
        remote(
            2,
            cache_lat.at[:, 0:2, pl.ds(lat_src, 96)],
            lat.at[:, 6:8, pl.ds(lat_dst, 96)],
            (ta, up),
        ),
        remote(3, cache_feat.at[:, 0, :, feat], cf_edge.at[1], (ta, up)),
    ]
    to_down = [
        remote(4, tokens.at[:, 1], tok.at[:, 0, own], (ta, down)),
        remote(
            5,
            tokens.at[:, 1, pl.ds(edge_src, HALO)],
            tok.at[:, 0, pl.ds(edge_dst, HALO)],
            (other, down),
        ),
        remote(
            6,
            cache_lat.at[:, 2:4, pl.ds(lat_src, 96)],
            lat.at[:, 0:2, pl.ds(lat_dst, 96)],
            (ta, down),
        ),
        remote(7, cache_feat.at[:, 7, :, feat], cf_edge.at[0], (ta, down)),
    ]
    beside = remote(
        8,
        tokens.at[:, :, pl.ds(edge_src, HALO)],
        tok.at[:, 1:3, pl.ds(edge_dst, HALO)],
        (other, ha),
    )

    local[2].wait()

    def build_first(dt, carry):
        for block in range(16):
            row_tap = ((block >> 1 & 1) + 2 * (block >> 2 & 1) + 1) % 4
            col_tap = ((block & 1) + 2 * (block >> 3) + 1) % 4
            for q in range(2):
                for r in range(2):
                    dr, dc = row_tap - q, col_tap - r
                    if 0 <= dr < 3 and 0 <= dc < 3:
                        piece = w_in[dt, dr, dc]
                    else:
                        piece = jnp.zeros((C0, C1), BF)
                    at = pl.ds(pl.multiple_of(dt * 256 + block * C0, C0), C0)
                    w1[q, at, r * C1 : (r + 1) * C1] = piece
        return carry

    lax.fori_loop(0, 3, build_first, 0)

    partners = 5 - 2 * top.astype(jnp.int32) - 2 * bottom.astype(jnp.int32)
    pl.semaphore_wait(barrier, partners)
    beside.start()

    @pl.when(jnp.logical_not(top))
    def _():
        for copy in to_up:
            copy.start()

    @pl.when(jnp.logical_not(bottom))
    def _():
        for copy in to_down:
            copy.start()

    @pl.when(left)
    def _():
        tok[:, :, 0:HALO] = jnp.zeros((4, 4, HALO, 4 * C0), BF)
        lat[:, :, 0:HALO] = jnp.zeros((2, 8, HALO, 2 * C0), BF)

    @pl.when(jnp.logical_not(left))
    def _():
        tok[:, :, HALO + PATCH_COLS :] = jnp.zeros((4, 4, HALO, 4 * C0), BF)
        lat[:, :, HALO + PATCH_COLS :] = jnp.zeros((2, 8, HALO, 2 * C0), BF)

    lane_f = lax.broadcasted_iota(jnp.int32, (PATCH_COLS, FEAT), 1)
    sub_f = lax.broadcasted_iota(jnp.int32, (PATCH_COLS, FEAT), 0)
    for b in range(6):
        hit = lane_f == 4 * sub_f + (b - 1) + 64 * ta
        pick[b * PATCH_COLS : (b + 1) * PATCH_COLS, :] = jnp.where(hit, 1.0, 0.0).astype(BF)

    local[4].wait()

    def cached_row(t, row, columns):
        res = lax.dot_general(
            pick[...], columns, (((1,), (1,)), ((), ())), preferred_element_type=F32
        )
        for b, ref in enumerate((fe, fo, fe1)):
            at = 2 * b * PATCH_COLS
            pair = jnp.concatenate(
                [res[at : at + PATCH_COLS], res[at + PATCH_COLS : at + 2 * PATCH_COLS]], axis=1
            )
            ref[t, row] = pair.astype(BF)

    def cached_own(t, carry):
        for row in range(1, 9):
            cached_row(t, row, cf[t, row - 1])
        return carry

    lax.fori_loop(0, 2, cached_own, 0)

    local[3].wait()
    taps = {(0, 0): (0, 1), (1, 0): (2,), (0, 1): (0,), (1, 1): (1, 2)}

    def total(parts):
        return functools.reduce(lambda x, y: x + y, parts)

    for kr in range(2):
        for pr in range(2):
            rows = [
                total([w_up[dr, dc].astype(F32) for dr in taps[kr, pr]]) for dc in range(3)
            ]
            for kc in range(2):
                for pc in range(2):
                    out_at = (2 * pr + pc) * C2
                    in_at = (2 * kr + kc) * C1
                    w2[out_at : out_at + C2, in_at : in_at + C1] = total(
                        [rows[dc] for dc in taps[kc, pc]]
                    ).astype(BF)

    local[5].wait()

    z = jnp.zeros((C2, C3), BF)
    for n in range(9):
        w = w_out[n]
        w3[n * 768 : (n + 1) * 768, :] = jnp.concatenate(
            [jnp.concatenate([w, z], axis=0), jnp.concatenate([z, w], axis=0)], axis=1
        )
    ws = w_skip[...]
    w3[9 * 768 : 9 * 768 + C2, :] = jnp.concatenate([z, ws], axis=1)
    w3[9 * 768 + C2 :, :] = jnp.concatenate([ws, z], axis=1)

    bias1 = b1[...].reshape(1, C1)
    gain1 = 0.5 * g1[...].reshape(1, C1)
    bias2 = jnp.concatenate([b2[...].reshape(1, C2)] * 2, axis=1)
    gain2 = 0.5 * jnp.concatenate([g2[...].reshape(1, C2)] * 2, axis=1)
    bias3 = jnp.concatenate([b3[...].reshape(1, C3)] * 4, axis=1)

    beside.wait_recv()
    local[0].wait()
    local[1].wait()

    @pl.when(top)
    def _():
        tok[:, 0] = jnp.zeros((4, TOK, 4 * C0), BF)
        lat[:, 0:2] = jnp.zeros((2, 2, TOK, 2 * C0), BF)
        cf_edge[0] = jnp.zeros((2, C2, FEAT), BF)

    @pl.when(jnp.logical_not(top))
    def _():
        for copy in to_down[:3]:
            copy.wait_recv()

    @pl.when(bottom)
    def _():
        tok[:, 3] = jnp.zeros((4, TOK, 4 * C0), BF)
        lat[:, 6:8] = jnp.zeros((2, 2, TOK, 2 * C0), BF)
        cf_edge[1] = jnp.zeros((2, C2, FEAT), BF)

    @pl.when(jnp.logical_not(bottom))
    def _():
        for copy in to_up[:3]:
            copy.wait_recv()

    lane64 = lax.broadcasted_iota(jnp.int32, (TOK, 4 * C0), 1)
    second_row = lane64 >= 2 * C0
    second_col = (lane64 // C0) % 2 == 1

    def windows(t, rows):
        for u in range(4):
            above = rows[max(u - 1, 0)]
            below = rows[min(u + 1, 3)]
            here = rows[u]
            vert = jnp.where(second_row, above, below)
            horiz = jnp.where(second_col, pltpu.roll(here, 1, 0), pltpu.roll(here, TOK - 1, 0))
            diag = jnp.where(second_col, pltpu.roll(vert, 1, 0), pltpu.roll(vert, TOK - 1, 0))
            full = jnp.concatenate([here, vert, horiz, diag], axis=1)
            win[t, u] = pltpu.roll(full, 1, 0)[HALO : HALO + WIDE].astype(BF)

    def cached_windows(t, carry):
        rows = [lat[t, n].astype(F32) for n in range(8)]
        windows(t, [jnp.concatenate(rows[2 * u : 2 * u + 2], axis=1) for u in range(4)])
        return carry

    def token_windows(t, carry):
        windows(t + 2, [tok[t, u].astype(F32) for u in range(4)])
        return carry

    lax.fori_loop(0, 2, cached_windows, 0)
    lax.fori_loop(0, 4, token_windows, 0)
    keep_top = jnp.where(top, 0.0, 1.0)
    keep_bottom = jnp.where(bottom, 0.0, 1.0)
    sub8 = lax.broadcasted_iota(jnp.int32, (8, 2 * C2), 0)
    lane8 = lax.broadcasted_iota(jnp.int32, (8, 2 * C2), 1)
    not_left = jnp.where(jnp.logical_and(sub8 == 0, left), 0.0, 1.0)
    keep_right = jnp.where(left, 1.0, 0.0)
    out_left = jnp.where(
        jnp.logical_and(jnp.logical_and(sub8 == 0, lane8 < C2), left), 0.0, 1.0
    )
    out_right = jnp.where(
        jnp.logical_and(jnp.logical_and(sub8 == 0, lane8 >= C2), jnp.logical_not(left)), 0.0, 1.0
    )

    for row in range(6):
        u, q = (row + 1) // 2, (row + 1) % 2
        y1 = (y1a, y1b)[row % 2]
        lhs = jnp.concatenate(
            [win[dt : dt + 4, u].reshape(4 * WIDE, 256) for dt in range(3)], axis=1
        )
        y1[...] = jnp.dot(lhs, w1[q], preferred_element_type=F32)
        for f in range(4):
            acts = []
            for r in range(2):
                v = y1[f * WIDE : (f + 1) * WIDE, r * C1 : (r + 1) * C1] + bias1
                scale = lax.rsqrt(jnp.mean(v * v, axis=1, keepdims=True) + 1e-06)
                act = silu_half(v * scale * gain1)
                if row == 0:
                    act = act * keep_top
                if row == 5:
                    act = act * keep_bottom
                acts.append(act)
            shifted = pltpu.roll(acts[0], WIDE - 1, 0)
            a_r0[f, row, :PATCH_COLS] = shifted[:PATCH_COLS].astype(BF)
            a_r0[f, row, PATCH_COLS:] = (shifted[PATCH_COLS:] * keep_right).astype(BF)
            a_r1p[f, row] = jnp.concatenate([acts[1][:8] * not_left, acts[1][8:]], axis=0).astype(
                BF
            )
            a_r1c[f, row] = pltpu.roll(acts[1], WIDE - 1, 0)[:PATCH_COLS].astype(BF)

    low_half = lax.broadcasted_iota(jnp.int32, (1, 128), 1) < 64

    def norm_pair(v):
        v0, v1, v2 = v[:, 0:128], v[:, 128:256], v[:, 256:384]
        sq1 = v1 * v1
        sum_a = jnp.sum(v0 * v0 + jnp.where(low_half, sq1, 0.0), axis=1, keepdims=True)
        sum_b = jnp.sum(v2 * v2 + jnp.where(low_half, 0.0, sq1), axis=1, keepdims=True)
        scale_a = lax.rsqrt(sum_a * (1.0 / C2) + 1e-06)
        scale_b = lax.rsqrt(sum_b * (1.0 / C2) + 1e-06)
        scaled = jnp.concatenate(
            [v0 * scale_a, v1 * jnp.where(low_half, scale_a, scale_b), v2 * scale_b], axis=1
        )
        return silu_half(scaled * gain2)

    first_col = lax.broadcasted_iota(jnp.int32, (1, 2 * C2), 1) < C2

    def second(f):
        lhs = jnp.concatenate(
            [a_r1p[f, 0:5], a_r0[f, 0:5], a_r1p[f, 1:6], a_r0[f, 1:6]], axis=2
        ).reshape(5 * WIDE, 4 * C1)
        y2e[...] = lax.dot_general(
            lhs, w2[...], (((1,), (1,)), ((), ())), preferred_element_type=F32
        )
        lhs = jnp.concatenate(
            [a_r0[f, 0:5, :PATCH_COLS], a_r1c[f, 0:5], a_r0[f, 1:6, :PATCH_COLS], a_r1c[f, 1:6]],
            axis=2,
        ).reshape(5 * PATCH_COLS, 4 * C1)
        y2o[...] = lax.dot_general(
            lhs, w2[...], (((1,), (1,)), ((), ())), preferred_element_type=F32
        )

        for row in range(10):
            i, par = row // 2, row % 2
            cols = slice(par * 384, (par + 1) * 384)
            ve = y2e[i * WIDE : i * WIDE + 88, cols] + bias2
            vo = y2o[i * PATCH_COLS : (i + 1) * PATCH_COLS, cols] + bias2
            act = norm_pair(ve)
            act_o = norm_pair(vo)
            if row == 0:
                act, act_o = act * keep_top, act_o * keep_top
            if row == 9:
                act, act_o = act * keep_bottom, act_o * keep_bottom
            act = jnp.concatenate(
                [act[:8] * out_left, act[8:PATCH_COLS], act[PATCH_COLS:] * out_right], axis=0
            )
            fe[f + 2, row] = act[:PATCH_COLS].astype(BF)
            fe1[f + 2, row] = pltpu.roll(act, 87, 0)[:PATCH_COLS].astype(BF)
            fo[f + 2, row] = act_o.astype(BF)
            if 1 <= row <= 8:
                ve1 = pltpu.roll(ve, 87, 0)[:PATCH_COLS]
                ue[f, row - 1] = jnp.where(first_col, vo, ve[:PATCH_COLS]).astype(BF)
                uo[f, row - 1] = jnp.where(first_col, ve1, vo).astype(BF)

    def third(f, acc):
        for y in (0, 4):
            blocks = []
            for dt in range(3):
                for dr in range(3):
                    part = slice(y + dr, y + dr + 4)
                    e, o, e1 = fe[f + dt, part], fo[f + dt, part], fe1[f + dt, part]
                    blocks.append(
                        jnp.concatenate(
                            [
                                jnp.concatenate([e, o], axis=2),
                                jnp.concatenate([o, e1], axis=2),
                            ],
                            axis=0,
                        ).reshape(8 * PATCH_COLS, 768)
                    )
            mine = slice(y, y + 4)
            blocks.append(
                jnp.concatenate([ue[f, mine], uo[f, mine]], axis=0).reshape(8 * PATCH_COLS, 384)
            )
            res = jnp.dot(jnp.concatenate(blocks, axis=1), w3[...], preferred_element_type=F32)
            half = 4 * PATCH_COLS
            both = jnp.concatenate([res[:half], res[half:]], axis=1)
            for piece in range(3):
                acc[piece, y * PATCH_COLS : y * PATCH_COLS + half, :] = both[
                    :, piece * 128 : (piece + 1) * 128
                ]

    def turn(f, acc):
        for s in range(PATCH_COLS):
            part = pl.ds(s, 8, stride=PATCH_COLS)
            x = jnp.concatenate([acc[piece, part, :] for piece in range(3)], axis=1) + bias3
            ostage[f, :, s * 384 : (s + 1) * 384] = x.astype(BF)

    def second_loop(f, carry):
        second(f)
        return carry

    lax.fori_loop(0, 3, second_loop, 0)

    @pl.when(jnp.logical_not(top))
    def _():
        to_down[3].wait_recv()

    @pl.when(jnp.logical_not(bottom))
    def _():
        to_up[3].wait_recv()

    for t in range(2):
        cached_row(t, 0, cf_edge[0, t])
        cached_row(t, 9, cf_edge[1, t])

    half_lanes = PATCH_COLS * 384
    lanes = pl.ds(pl.multiple_of(ta * half_lanes, 128), half_lanes)

    def sent(k):
        f = 2 * other + k
        return remote(9 + k, ostage.at[f], out.at[k, :, lanes], (other, ha))

    def kept(k):
        f = 2 * ta + k
        return pltpu.make_async_copy(ostage.at[f], out.at[k, :, lanes], local_sem.at[6 + k])

    third(2 * other, acc_a)
    turn(2 * other, acc_a)
    sent(0).start()
    second(3)
    third(2 * other + 1, acc_b)
    turn(2 * other + 1, acc_b)
    sent(1).start()
    third(2 * ta, acc_a)
    turn(2 * ta, acc_a)
    kept(0).start()
    third(2 * ta + 1, acc_b)
    turn(2 * ta + 1, acc_b)
    kept(1).start()
    beside.wait_send()

    @pl.when(jnp.logical_not(top))
    def _():
        for copy in to_up:
            copy.wait_send()

    @pl.when(jnp.logical_not(bottom))
    def _():
        for copy in to_down:
            copy.wait_send()

    for k in range(2):
        kept(k).wait()
    for k in range(2):
        sent(k).wait()


def shards(
    tokens,
    cache_latent,
    cache_feature,
    weight_in,
    weight_up,
    weight_out,
    weight_skip,
    bias_in,
    bias_up,
    bias_out,
    gain_in,
    gain_up,
):
    tok = tokens.reshape(4, 2, PATCH_COLS, 4 * C0)
    lat = cache_latent.reshape(2, 4, 160, 2 * C0)
    any_spec = pl.BlockSpec(memory_space=pl.ANY)
    vmem = pl.BlockSpec(memory_space=pltpu.VMEM)
    scratch = [
        pltpu.VMEM((4, 4, TOK, 4 * C0), BF),
        pltpu.VMEM((2, 8, TOK, 2 * C0), BF),
        pltpu.VMEM((6, 4, WIDE, 256), BF),
        pltpu.VMEM((4 * WIDE, 2 * C1), F32),
        pltpu.VMEM((4 * WIDE, 2 * C1), F32),
        pltpu.VMEM((4, 6, WIDE, C1), BF),
        pltpu.VMEM((4, 6, WIDE, C1), BF),
        pltpu.VMEM((4, 6, PATCH_COLS, C1), BF),
        pltpu.VMEM((5 * WIDE, 4 * C2), F32),
        pltpu.VMEM((5 * PATCH_COLS, 4 * C2), F32),
        pltpu.VMEM((6, 10, PATCH_COLS, 2 * C2), BF),
        pltpu.VMEM((6, 10, PATCH_COLS, 2 * C2), BF),
        pltpu.VMEM((6, 10, PATCH_COLS, 2 * C2), BF),
        pltpu.VMEM((4, 8, PATCH_COLS, 2 * C2), BF),
        pltpu.VMEM((4, 8, PATCH_COLS, 2 * C2), BF),
        pltpu.VMEM((2, 8, C2, FEAT), BF),
        pltpu.VMEM((2, 2, C2, FEAT), BF),
        pltpu.VMEM((6 * PATCH_COLS, FEAT), BF),
        pltpu.VMEM((3, 8 * PATCH_COLS, 128), F32),
        pltpu.VMEM((3, 8 * PATCH_COLS, 128), F32),
        pltpu.VMEM((4, 8, PATCH_COLS * 384), BF),
        pltpu.VMEM((3, 3, 3, C0, C1), BF),
        pltpu.VMEM((3, 3, C2, C1), BF),
        pltpu.VMEM((9, 3 * C2, C3), BF),
        pltpu.VMEM((2, 768, 2 * C1), BF),
        pltpu.VMEM((4 * C2, 4 * C1), BF),
        pltpu.VMEM((9 * 768 + 384, 2 * C3), BF),
        pltpu.SemaphoreType.DMA((11,)),
        pltpu.SemaphoreType.DMA((11,)),
        pltpu.SemaphoreType.DMA((8,)),
    ]
    return pl.pallas_call(
        kernel,
        out_shape=jax.ShapeDtypeStruct((2, 8, 640 * C3), BF),
        in_specs=[any_spec] * 6 + [vmem] * 6,
        out_specs=any_spec,
        scratch_shapes=scratch,
        compiler_params=pltpu.CompilerParams(
            collective_id=0, has_side_effects=True, vmem_limit_bytes=60 * 1024 * 1024
        ),
        cost_estimate=pl.CostEstimate(
            flops=28_000_000_000, bytes_accessed=16_000_000, transcendentals=5_000_000
        ),
    )(
        tok,
        lat,
        cache_feature.transpose(0, 1, 3, 2),
        weight_in,
        weight_up.transpose(0, 1, 3, 2),
        weight_out.reshape(9, 3 * C2, C3),
        weight_skip,
        bias_in,
        bias_up,
        bias_out,
        gain_in,
        gain_up,
    )


def solution(mesh):
    placed = (
        P(None, "ha", "ta"),
        P(None, "ha", None),
        P(None, "ha", None, None),
        P(),
        P(),
        P(),
        P(),
        P(),
        P(),
        P(),
        P(),
        P(),
    )
    return jax.shard_map(
        shards, mesh=mesh, in_specs=placed, out_specs=P("ta", "ha", None), check_vma=False
    )
```

time: 140 us -> 64.3 us (0.46)
  the two profiles are of different devices: /device:TPU:0 before, /device:TPU:24 now
where the time goes in v2:
time: 64.3 us; the launch traced here: 64 us
  Pallas kernels  53.8 us (84%)
  local copies, waits for them, and re-layouts  10.2 us (16%)
    pallas_call x1, Pallas kernels, shards(): pl.pallas_call(kernel, out_shape=jax.ShapeDtypeStruct((2, 8, 640 * C3), B...  53.8 us
    reshape x1, local copies, waits for them, and re-layouts, shards(): weight_out.reshape(9, 3 * C2, C3)  3.72 us
    unnamed x1, local copies, waits for them, and re-layouts  2.94 us
    reshape x1, local copies, waits for them, and re-layouts, shards(): lat = cache_latent.reshape(2, 4, 160, 2 * C0)  1.85 us
    reshape x1, local copies, waits for them, and re-layouts, shards(): tok = tokens.reshape(4, 2, PATCH_COLS, 4 * C0)  1.71 us

profile of v2, /device:TPU:24, one launch (start us, length us, event | category | flops | bytes accessed | tf_op | source)
XLA Modules:
  0.0 64.0 jit_solution(7090686324859017243)
XLA Ops:
  0.0 1.7 %reshape.9.tokens = bf16[4,2,80,64]{3,2,1,0:T(8,128)(2,1)} reshape(bf16[4,2,5120]{2,1,0:T(2,128)(2,1)} %param.12) | data formatting | bytes 163840 | tf_op jit(solution)/shard_map/reshape | solution.py:531
  1.7 1.9 %reshape.10.cache_lat = bf16[2,4,160,32]{3,2,1,0:T(8,128)(2,1)} reshape(bf16[2,4,5120]{2,1,0:T(4,128)(2,1)} %param.13) | data formatting | bytes 163840 | tf_op jit(solution)/shard_map/reshape | solution.py:532
  3.6 3.7 %reshape.11.w_out_hbm = bf16[9,576,96]{2,1,0:T(8,128)(2,1)} reshape(bf16[3,3,3,18432]{3,2,1,0:T(4,128)(2,1)} %param.17) | data formatting | bytes 1990656 | tf_op jit(solution)/shard_map/reshape | solution.py:585
  7.3 53.8 %shard_map.118 = bf16[2,8,61440]{2,1,0:T(8,128)(2,1)} custom-call(bf16[4,2,80,64]{3,2,1,0:T(8,128)(2,1)} %reshape.9.tokens, bf16[2,4,160,32]{3,2,1,0:T(8,128)(2,1)} %reshape.10.cache_lat, bf16[2,8,192,640]{3,2,1,0:T(8,128)(2,1)} %bitcast.2, bf16[3,3,3,16,384]{4,3,2,1,0:T(8,128)(2,1)} %w_in_hbm.1, bf16[3,3,192,384]{3,2,1,0:T(8,128)(2,1)} %bitcast.3, ...), custom_call_target="tpu_custom_call" | custom-call | flops 28000000000 | bytes 16000000 | tf_op jit(solution)/shard_map/pallas_call | solution.py:567
  61.1 2.9 %copy.14 = bf16[2,8,61440]{2,1,0:T(8,128)(2,1)} copy(bf16[2,8,61440]{2,1,0:T(8,128)(2,1)} %shard_map.118) | data formatting | bytes 3932160

commit v3 on v2

--- a/solution.py
+++ b/solution.py
@@ -280,34 +280,12 @@
     local[0].wait()
     local[1].wait()
 
-    @pl.when(top)
-    def _():
-        tok[:, 0] = jnp.zeros((4, TOK, 4 * C0), BF)
-        lat[:, 0:2] = jnp.zeros((2, 2, TOK, 2 * C0), BF)
-        cf_edge[0] = jnp.zeros((2, C2, FEAT), BF)
-
-    @pl.when(jnp.logical_not(top))
-    def _():
-        for copy in to_down[:3]:
-            copy.wait_recv()
-
-    @pl.when(bottom)
-    def _():
-        tok[:, 3] = jnp.zeros((4, TOK, 4 * C0), BF)
-        lat[:, 6:8] = jnp.zeros((2, 2, TOK, 2 * C0), BF)
-        cf_edge[1] = jnp.zeros((2, C2, FEAT), BF)
-
-    @pl.when(jnp.logical_not(bottom))
-    def _():
-        for copy in to_up[:3]:
-            copy.wait_recv()
-
     lane64 = lax.broadcasted_iota(jnp.int32, (TOK, 4 * C0), 1)
     second_row = lane64 >= 2 * C0
     second_col = (lane64 // C0) % 2 == 1
 
-    def windows(t, rows):
-        for u in range(4):
+    def windows(t, rows, which):
+        for u in which:
             above = rows[max(u - 1, 0)]
             below = rows[min(u + 1, 3)]
             here = rows[u]
@@ -317,17 +295,33 @@
             full = jnp.concatenate([here, vert, horiz, diag], axis=1)
             win[t, u] = pltpu.roll(full, 1, 0)[HALO : HALO + WIDE].astype(BF)
 
-    def cached_windows(t, carry):
-        rows = [lat[t, n].astype(F32) for n in range(8)]
-        windows(t, [jnp.concatenate(rows[2 * u : 2 * u + 2], axis=1) for u in range(4)])
-        return carry
-
-    def token_windows(t, carry):
-        windows(t + 2, [tok[t, u].astype(F32) for u in range(4)])
-        return carry
-
-    lax.fori_loop(0, 2, cached_windows, 0)
-    lax.fori_loop(0, 4, token_windows, 0)
+    def cached_rows(t, u):
+        return jnp.concatenate(
+            [lat[t, 2 * u].astype(F32), lat[t, 2 * u + 1].astype(F32)], axis=1
+        )
+
+    def token_rows(t, u):
+        return tok[t, u].astype(F32)
+
+    def inner_windows(t, get, base):
+        first, last = get(t, 1), get(t, 2)
+        windows(t + base, [first, first, last, last], (1, 2))
+
+    def all_windows(t, get, base):
+        windows(t + base, [get(t, u) for u in range(4)], range(4))
+
+    def each_frame(work):
+        def cached_frame(t, carry):
+            work(t, cached_rows, 0)
+            return carry
+
+        def token_frame(t, carry):
+            work(t, token_rows, 2)
+            return carry
+
+        lax.fori_loop(0, 2, cached_frame, 0)
+        lax.fori_loop(0, 4, token_frame, 0)
+
     keep_top = jnp.where(top, 0.0, 1.0)
     keep_bottom = jnp.where(bottom, 0.0, 1.0)
     sub8 = lax.broadcasted_iota(jnp.int32, (8, 2 * C2), 0)
@@ -341,7 +335,7 @@
         jnp.logical_and(jnp.logical_and(sub8 == 0, lane8 >= C2), jnp.logical_not(left)), 0.0, 1.0
     )
 
-    for row in range(6):
+    def first(row):
         u, q = (row + 1) // 2, (row + 1) % 2
         y1 = (y1a, y1b)[row % 2]
         lhs = jnp.concatenate(
@@ -383,26 +377,28 @@
 
     first_col = lax.broadcasted_iota(jnp.int32, (1, 2 * C2), 1) < C2
 
-    def second(f):
-        lhs = jnp.concatenate(
-            [a_r1p[f, 0:5], a_r0[f, 0:5], a_r1p[f, 1:6], a_r0[f, 1:6]], axis=2
-        ).reshape(5 * WIDE, 4 * C1)
-        y2e[...] = lax.dot_general(
-            lhs, w2[...], (((1,), (1,)), ((), ())), preferred_element_type=F32
-        )
-        lhs = jnp.concatenate(
-            [a_r0[f, 0:5, :PATCH_COLS], a_r1c[f, 0:5], a_r0[f, 1:6, :PATCH_COLS], a_r1c[f, 1:6]],
-            axis=2,
-        ).reshape(5 * PATCH_COLS, 4 * C1)
-        y2o[...] = lax.dot_general(
-            lhs, w2[...], (((1,), (1,)), ((), ())), preferred_element_type=F32
-        )
-
-        for row in range(10):
-            i, par = row // 2, row % 2
+    def second_products(at_f, spans, even_rows, odd_rows):
+        def window(refs, stop):
+            parts = []
+            for lo, hi in spans:
+                pieces = [ref[at_f, lo + down : hi + down, 0:stop] for down in (0, 1) for ref in refs]
+                parts.append(jnp.concatenate(pieces, axis=-1).reshape(-1, 4 * C1))
+            return jnp.concatenate(parts, axis=0)
+
+        for rows, refs, y2, stop in (
+            (even_rows, (a_r1p, a_r0), y2e, WIDE),
+            (odd_rows, (a_r0, a_r1c), y2o, PATCH_COLS),
+        ):
+            y2[0:rows] = lax.dot_general(
+                window(refs, stop), w2[...], (((1,), (1,)), ((), ())), preferred_element_type=F32
+            )
+
+    def second_finish(f, i, at):
+        for par in range(2):
+            row = 2 * i + par
             cols = slice(par * 384, (par + 1) * 384)
-            ve = y2e[i * WIDE : i * WIDE + 88, cols] + bias2
-            vo = y2o[i * PATCH_COLS : (i + 1) * PATCH_COLS, cols] + bias2
+            ve = y2e[at * WIDE : at * WIDE + 88, cols] + bias2
+            vo = y2o[at * PATCH_COLS : (at + 1) * PATCH_COLS, cols] + bias2
             act = norm_pair(ve)
             act_o = norm_pair(vo)
             if row == 0:
@@ -420,39 +416,70 @@
                 ue[f, row - 1] = jnp.where(first_col, vo, ve[:PATCH_COLS]).astype(BF)
                 uo[f, row - 1] = jnp.where(first_col, ve1, vo).astype(BF)
 
-    def third(f, acc):
+    def second(f):
+        second_products(f, ((0, 2), (3, 5)), 4 * WIDE, 4 * PATCH_COLS)
+        for at, i in enumerate((0, 1, 3, 4)):
+            second_finish(f, i, at)
+
+    each_frame(inner_windows)
+    first(2)
+    first(3)
+    second_products(slice(0, 4), ((2, 3),), 4 * WIDE, 4 * PATCH_COLS)
+    for f in range(4):
+        second_finish(f, 2, f)
+
+    @pl.when(top)
+    def _():
+        tok[:, 0] = jnp.zeros((4, TOK, 4 * C0), BF)
+        lat[:, 0:2] = jnp.zeros((2, 2, TOK, 2 * C0), BF)
+        cf_edge[0] = jnp.zeros((2, C2, FEAT), BF)
+
+    @pl.when(jnp.logical_not(top))
+    def _():
+        for copy in to_down[:3]:
+            copy.wait_recv()
+
+    @pl.when(bottom)
+    def _():
+        tok[:, 3] = jnp.zeros((4, TOK, 4 * C0), BF)
+        lat[:, 6:8] = jnp.zeros((2, 2, TOK, 2 * C0), BF)
+        cf_edge[1] = jnp.zeros((2, C2, FEAT), BF)
+
+    @pl.when(jnp.logical_not(bottom))
+    def _():
+        for copy in to_up[:3]:
+            copy.wait_recv()
+
+    each_frame(all_windows)
+    for row in (0, 1, 4, 5):
+        first(row)
+
+    def third(f, start, n, acc):
+        at = slice(start, start + n)
         for y in (0, 4):
-            blocks = []
+            parts = []
             for dt in range(3):
                 for dr in range(3):
-                    part = slice(y + dr, y + dr + 4)
-                    e, o, e1 = fe[f + dt, part], fo[f + dt, part], fe1[f + dt, part]
-                    blocks.append(
+                    rows = slice(y + dr, y + dr + 4)
+                    e, o, e1 = fe[f + dt, rows, at], fo[f + dt, rows, at], fe1[f + dt, rows, at]
+                    parts.append(
                         jnp.concatenate(
-                            [
-                                jnp.concatenate([e, o], axis=2),
-                                jnp.concatenate([o, e1], axis=2),
-                            ],
+                            [jnp.concatenate([e, o], axis=2), jnp.concatenate([o, e1], axis=2)],
                             axis=0,
-                        ).reshape(8 * PATCH_COLS, 768)
+                        ).reshape(8 * n, 768)
                     )
             mine = slice(y, y + 4)
-            blocks.append(
-                jnp.concatenate([ue[f, mine], uo[f, mine]], axis=0).reshape(8 * PATCH_COLS, 384)
+            parts.append(
+                jnp.concatenate([ue[f, mine, at], uo[f, mine, at]], axis=0).reshape(8 * n, 384)
             )
-            res = jnp.dot(jnp.concatenate(blocks, axis=1), w3[...], preferred_element_type=F32)
-            half = 4 * PATCH_COLS
-            both = jnp.concatenate([res[:half], res[half:]], axis=1)
+            res = jnp.dot(jnp.concatenate(parts, axis=1), w3[...], preferred_element_type=F32)
+            both = jnp.concatenate([res[: 4 * n], res[4 * n :]], axis=1)
             for piece in range(3):
-                acc[piece, y * PATCH_COLS : y * PATCH_COLS + half, :] = both[
-                    :, piece * 128 : (piece + 1) * 128
-                ]
-
-    def turn(f, acc):
-        for s in range(PATCH_COLS):
-            part = pl.ds(s, 8, stride=PATCH_COLS)
+                acc[piece, y * n : (y + 4) * n, :] = both[:, piece * 128 : (piece + 1) * 128]
+        for s in range(n):
+            part = pl.ds(s, 8, stride=n)
             x = jnp.concatenate([acc[piece, part, :] for piece in range(3)], axis=1) + bias3
-            ostage[f, :, s * 384 : (s + 1) * 384] = x.astype(BF)
+            ostage[f, :, (start + s) * 384 : (start + s + 1) * 384] = x.astype(BF)
 
     def second_loop(f, carry):
         second(f)
@@ -475,26 +502,32 @@
     half_lanes = PATCH_COLS * 384
     lanes = pl.ds(pl.multiple_of(ta * half_lanes, 128), half_lanes)
 
-    def sent(k):
+    def sent(slot, k, start, n):
         f = 2 * other + k
-        return remote(9 + k, ostage.at[f], out.at[k, :, lanes], (other, ha))
+        there = pl.ds(pl.multiple_of(ta * half_lanes + start * 384, 128), n * 384)
+        return remote(
+            slot,
+            ostage.at[f, :, start * 384 : (start + n) * 384],
+            out.at[k, :, there],
+            (other, ha),
+        )
+
+    sends = [sent(9, 0, 0, 48), sent(10, 0, 48, 32), sent(11, 1, 0, PATCH_COLS)]
 
     def kept(k):
         f = 2 * ta + k
         return pltpu.make_async_copy(ostage.at[f], out.at[k, :, lanes], local_sem.at[6 + k])
 
-    third(2 * other, acc_a)
-    turn(2 * other, acc_a)
-    sent(0).start()
+    third(2 * other, 0, 48, acc_a)
+    sends[0].start()
+    third(2 * other, 48, 32, acc_b)
+    sends[1].start()
     second(3)
-    third(2 * other + 1, acc_b)
-    turn(2 * other + 1, acc_b)
-    sent(1).start()
-    third(2 * ta, acc_a)
-    turn(2 * ta, acc_a)
+    third(2 * other + 1, 0, PATCH_COLS, acc_a)
+    sends[2].start()
+    third(2 * ta, 0, PATCH_COLS, acc_b)
     kept(0).start()
-    third(2 * ta + 1, acc_b)
-    turn(2 * ta + 1, acc_b)
+    third(2 * ta + 1, 0, PATCH_COLS, acc_a)
     kept(1).start()
     beside.wait_send()
 
@@ -510,8 +543,39 @@
 
     for k in range(2):
         kept(k).wait()
-    for k in range(2):
-        sent(k).wait()
+    for copy in sends:
+        copy.wait()
+
+
+def copied(x):
+    def body(src, dst, buf, sem_in, sem_out):
+        size = 15360
+        into, back = [], []
+        for k in range(2):
+            for n in range(4):
+                at = slice(n * size, (n + 1) * size)
+                into.append(pltpu.make_async_copy(src.at[k, :, at], buf.at[k, :, at], sem_in.at[k, n]))
+                back.append(pltpu.make_async_copy(buf.at[k, :, at], dst.at[k, :, at], sem_out.at[k, n]))
+        for copy in into:
+            copy.start()
+        for copy, after in zip(into, back):
+            copy.wait()
+            after.start()
+        for copy in back:
+            copy.wait()
+
+    spec = pl.BlockSpec(memory_space=pl.ANY)
+    return pl.pallas_call(
+        body,
+        out_shape=jax.ShapeDtypeStruct(x.shape, x.dtype),
+        in_specs=[spec],
+        out_specs=spec,
+        scratch_shapes=[
+            pltpu.VMEM(x.shape, BF),
+            pltpu.SemaphoreType.DMA((2, 4)),
+            pltpu.SemaphoreType.DMA((2, 4)),
+        ],
+    )(x)
 
 
 def shards(
@@ -560,18 +624,18 @@
         pltpu.VMEM((2, 768, 2 * C1), BF),
         pltpu.VMEM((4 * C2, 4 * C1), BF),
         pltpu.VMEM((9 * 768 + 384, 2 * C3), BF),
-        pltpu.SemaphoreType.DMA((11,)),
-        pltpu.SemaphoreType.DMA((11,)),
+        pltpu.SemaphoreType.DMA((12,)),
+        pltpu.SemaphoreType.DMA((12,)),
         pltpu.SemaphoreType.DMA((8,)),
     ]
-    return pl.pallas_call(
+    return copied(pl.pallas_call(
         kernel,
         out_shape=jax.ShapeDtypeStruct((2, 8, 640 * C3), BF),
         in_specs=[any_spec] * 6 + [vmem] * 6,
         out_specs=any_spec,
         scratch_shapes=scratch,
         compiler_params=pltpu.CompilerParams(
-            collective_id=0, has_side_effects=True, vmem_limit_bytes=60 * 1024 * 1024
+            collective_id=0, has_side_effects=True, vmem_limit_bytes=52 * 1024 * 1024
         ),
         cost_estimate=pl.CostEstimate(
             flops=28_000_000_000, bytes_accessed=16_000_000, transcendentals=5_000_000
@@ -589,7 +653,7 @@
         bias_out,
         gain_in,
         gain_up,
-    )
+    ))
 
 
 def solution(mesh):

time: 64.3 us -> 60.2 us (0.936)
  local copies, waits for them, and re-layouts: 10.2 us -> 5.99 us
    unnamed x1 -> x14, local copies, waits for them, and re-layouts: 2.94 us -> 0.03 us
    pallas_call x1, Pallas kernels: 53.8 us -> 51.2 us  [shards(): pl.pallas_call(kernel, out_shape=jax.ShapeDtypeStruct((2, 8, 640 * C3), B...]
    pallas_call x0 -> x1, Pallas kernels: none -> 2.47 us  [copied(): pl.pallas_call(body, out_shape=jax.ShapeDtypeStruct(x.shape, x.dtype), in...]
    reshape x1, local copies, waits for them, and re-layouts: 1.85 us -> 1.12 us  [shards(): lat = cache_latent.reshape(2, 4, 160, 2 * C0)]
where the time goes in v3:
time: 60.2 us; the launch traced here: 60 us
  Pallas kernels  53.7 us (89%)
  local copies, waits for them, and re-layouts  5.99 us (10%)
    pallas_call x1, Pallas kernels, shards(): pl.pallas_call(kernel, out_shape=jax.ShapeDtypeStruct((2, 8, 640 * C3), B...  51.2 us
    reshape x1, local copies, waits for them, and re-layouts, shards(): weight_out.reshape(9, 3 * C2, C3)  3.73 us
    pallas_call x1, Pallas kernels, copied(): pl.pallas_call(body, out_shape=jax.ShapeDtypeStruct(x.shape, x.dtype), in...  2.47 us

profile of v3, /device:TPU:24, one launch (start us, length us, event | category | flops | bytes accessed | tf_op | source)
XLA Modules:
  0.0 60.0 jit_solution(3129260975781248893)
XLA Ops:
  0.0 0.0 copy-start.5
  0.0 0.0 copy-start.3
  0.0 0.0 copy-start.6
  0.0 0.0 copy-start.4
  0.0 0.0 copy-start.2
  0.0 0.0 copy-start.1
  0.0 0.0 copy-start
  0.0 1.1 %reshape.9.tokens = bf16[4,2,80,64]{3,2,1,0:T(8,128)(2,1)S(1)} reshape(bf16[4,2,5120]{2,1,0:T(2,128)(2,1)} %param.12) | data formatting | bytes 163840 | tf_op jit(solution)/shard_map/reshape | solution.py:595
  1.2 1.1 %reshape.10.cache_lat = bf16[2,4,160,32]{3,2,1,0:T(8,128)(2,1)S(1)} reshape(bf16[2,4,5120]{2,1,0:T(4,128)(2,1)} %param.13) | data formatting | bytes 163840 | tf_op jit(solution)/shard_map/reshape | solution.py:596
  2.3 3.7 %reshape.11.w_out_hbm = bf16[9,576,96]{2,1,0:T(8,128)(2,1)} reshape(bf16[3,3,3,18432]{3,2,1,0:T(4,128)(2,1)} %param.17) | data formatting | bytes 1990656 | tf_op jit(solution)/shard_map/reshape | solution.py:649
  6.0 0.0 copy-done.5
  6.0 0.0 copy-done.3
  6.0 0.0 copy-done.6
  6.0 0.0 copy-done.4
  6.0 0.0 copy-done.2
  6.1 0.0 copy-done.1
  6.1 0.0 copy-done
  6.1 51.2 %shard_map.118.src = bf16[2,8,61440]{2,1,0:T(8,128)(2,1)} custom-call(bf16[4,2,80,64]{3,2,1,0:T(8,128)(2,1)S(1)} %reshape.9.tokens, bf16[2,4,160,32]{3,2,1,0:T(8,128)(2,1)S(1)} %reshape.10.cache_lat, bf16[2,8,192,640]{3,2,1,0:T(8,128)(2,1)} %bitcast.2, bf16[3,3,3,16,384]{4,3,2,1,0:T(8,128)(2,1)S(1)} %copy-done, bf16[3,3,192,384]{3,2,1,0:T(8,128)(2,1)} %bitcast.3, ...), custom_call_target="tpu_custom_call" | custom-call | flops 28000000000 | bytes 16000000 | tf_op jit(solution)/shard_map/pallas_call | solution.py:631
  57.3 2.5 %shard_map.119 = bf16[2,8,61440]{2,1,0:T(8,128)(2,1)} custom-call(bf16[2,8,61440]{2,1,0:T(8,128)(2,1)} %shard_map.118.src), custom_call_target="tpu_custom_call" | custom-call | tf_op jit(solution)/shard_map/pallas_call | solution.py:568
Async XLA Ops:
  0.0 6.0 %copy-start.5 = (f32[192]{0:T(256)S(1)}, f32[192]{0:T(256)}, u32[]{:S(2)}) copy-start(f32[192]{0:T(256)} %g2.1) | copy-start | bytes 2308
  0.0 6.0 %copy-start.3 = (f32[384]{0:T(512)S(1)}, f32[384]{0:T(512)}, u32[]{:S(2)}) copy-start(f32[384]{0:T(512)} %g1.1) | copy-start | bytes 4612
  0.0 6.0 %copy-start.6 = (f32[96]{0:T(128)S(1)}, f32[96]{0:T(128)}, u32[]{:S(2)}) copy-start(f32[96]{0:T(128)} %b3.1) | copy-start | bytes 1156
  0.0 6.0 %copy-start.4 = (f32[192]{0:T(256)S(1)}, f32[192]{0:T(256)}, u32[]{:S(2)}) copy-start(f32[192]{0:T(256)} %b2.1) | copy-start | bytes 2308
  0.0 6.0 %copy-start.2 = (f32[384]{0:T(512)S(1)}, f32[384]{0:T(512)}, u32[]{:S(2)}) copy-start(f32[384]{0:T(512)} %b1.1) | copy-start | bytes 4612
  0.0 6.0 %copy-start.1 = (bf16[192,96]{1,0:T(8,128)(2,1)S(1)}, bf16[192,96]{1,0:T(8,128)(2,1)}, u32[]{:S(2)}) copy-start(bf16[192,96]{1,0:T(8,128)(2,1)} %w_skip.1) | copy-start | bytes 110596
  0.0 6.0 %copy-start = (bf16[3,3,3,16,384]{4,3,2,1,0:T(8,128)(2,1)S(1)}, bf16[3,3,3,16,384]{4,3,2,1,0:T(8,128)(2,1)}, u32[]{:S(2)}) copy-start(bf16[3,3,3,16,384]{4,3,2,1,0:T(8,128)(2,1)} %w_in_hbm.1) | copy-start | bytes 995332

commit v4 on v3

--- a/solution.py
+++ b/solution.py
@@ -377,7 +377,7 @@
 
     first_col = lax.broadcasted_iota(jnp.int32, (1, 2 * C2), 1) < C2
 
-    def second_products(at_f, spans, even_rows, odd_rows):
+    def second_products(at_f, spans, even_rows, odd_rows, held):
         def window(refs, stop):
             parts = []
             for lo, hi in spans:
@@ -386,19 +386,19 @@
             return jnp.concatenate(parts, axis=0)
 
         for rows, refs, y2, stop in (
-            (even_rows, (a_r1p, a_r0), y2e, WIDE),
-            (odd_rows, (a_r0, a_r1c), y2o, PATCH_COLS),
+            (even_rows, (a_r1p, a_r0), held[0], WIDE),
+            (odd_rows, (a_r0, a_r1c), held[1], PATCH_COLS),
         ):
             y2[0:rows] = lax.dot_general(
                 window(refs, stop), w2[...], (((1,), (1,)), ((), ())), preferred_element_type=F32
             )
 
-    def second_finish(f, i, at):
+    def second_finish(f, i, at, held):
         for par in range(2):
             row = 2 * i + par
             cols = slice(par * 384, (par + 1) * 384)
-            ve = y2e[at * WIDE : at * WIDE + 88, cols] + bias2
-            vo = y2o[at * PATCH_COLS : (at + 1) * PATCH_COLS, cols] + bias2
+            ve = held[0][at * WIDE : at * WIDE + 88, cols] + bias2
+            vo = held[1][at * PATCH_COLS : (at + 1) * PATCH_COLS, cols] + bias2
             act = norm_pair(ve)
             act_o = norm_pair(vo)
             if row == 0:
@@ -417,16 +417,17 @@
                 uo[f, row - 1] = jnp.where(first_col, ve1, vo).astype(BF)
 
     def second(f):
-        second_products(f, ((0, 2), (3, 5)), 4 * WIDE, 4 * PATCH_COLS)
+        held = ((y2e, y2o), (y1a, y1b))[f % 2]
+        second_products(f, ((0, 2), (3, 5)), 4 * WIDE, 4 * PATCH_COLS, held)
         for at, i in enumerate((0, 1, 3, 4)):
-            second_finish(f, i, at)
+            second_finish(f, i, at, held)
 
     each_frame(inner_windows)
     first(2)
     first(3)
-    second_products(slice(0, 4), ((2, 3),), 4 * WIDE, 4 * PATCH_COLS)
+    second_products(slice(0, 4), ((2, 3),), 4 * WIDE, 4 * PATCH_COLS, (y2e, y2o))
     for f in range(4):
-        second_finish(f, 2, f)
+        second_finish(f, 2, f, (y2e, y2o))
 
     @pl.when(top)
     def _():
@@ -450,7 +451,10 @@
         for copy in to_up[:3]:
             copy.wait_recv()
 
-    each_frame(all_windows)
+    for t in range(2):
+        all_windows(t, cached_rows, 0)
+    for t in range(4):
+        all_windows(t, token_rows, 2)
     for row in (0, 1, 4, 5):
         first(row)
 
@@ -481,11 +485,8 @@
             x = jnp.concatenate([acc[piece, part, :] for piece in range(3)], axis=1) + bias3
             ostage[f, :, (start + s) * 384 : (start + s + 1) * 384] = x.astype(BF)
 
-    def second_loop(f, carry):
+    for f in range(3):
         second(f)
-        return carry
-
-    lax.fori_loop(0, 3, second_loop, 0)
 
     @pl.when(jnp.logical_not(top))
     def _():
@@ -605,8 +606,8 @@
         pltpu.VMEM((4, 6, WIDE, C1), BF),
         pltpu.VMEM((4, 6, WIDE, C1), BF),
         pltpu.VMEM((4, 6, PATCH_COLS, C1), BF),
-        pltpu.VMEM((5 * WIDE, 4 * C2), F32),
-        pltpu.VMEM((5 * PATCH_COLS, 4 * C2), F32),
+        pltpu.VMEM((4 * WIDE, 4 * C2), F32),
+        pltpu.VMEM((4 * PATCH_COLS, 4 * C2), F32),
         pltpu.VMEM((6, 10, PATCH_COLS, 2 * C2), BF),
         pltpu.VMEM((6, 10, PATCH_COLS, 2 * C2), BF),
         pltpu.VMEM((6, 10, PATCH_COLS, 2 * C2), BF),

time: 60.2 us -> 59 us (0.980)
  Pallas kernels: 53.7 us -> 52.4 us
    pallas_call x1, Pallas kernels: 51.2 us -> 50 us  [shards(): pl.pallas_call(kernel, out_shape=jax.ShapeDtypeStruct((2, 8, 640 * C3), B...]
where the time goes in v4:
time: 59 us; the launch traced here: 58.7 us
  Pallas kernels  52.4 us (89%)
  local copies, waits for them, and re-layouts  5.99 us (10%)
    pallas_call x1, Pallas kernels, shards(): pl.pallas_call(kernel, out_shape=jax.ShapeDtypeStruct((2, 8, 640 * C3), B...  50 us
    reshape x1, local copies, waits for them, and re-layouts, shards(): weight_out.reshape(9, 3 * C2, C3)  3.73 us
    pallas_call x1, Pallas kernels, copied(): pl.pallas_call(body, out_shape=jax.ShapeDtypeStruct(x.shape, x.dtype), in...  2.47 us

profile of v4, /device:TPU:24, one launch (start us, length us, event | category | flops | bytes accessed | tf_op | source)
XLA Modules:
  0.0 58.7 jit_solution(3907029143432866190)
XLA Ops:
  0.0 0.0 copy-start.5
  0.0 0.0 copy-start.3
  0.0 0.0 copy-start.6
  0.0 0.0 copy-start.4
  0.0 0.0 copy-start.2
  0.0 0.0 copy-start.1
  0.0 0.0 copy-start
  0.0 1.1 %reshape.9.tokens = bf16[4,2,80,64]{3,2,1,0:T(8,128)(2,1)S(1)} reshape(bf16[4,2,5120]{2,1,0:T(2,128)(2,1)} %param.12) | data formatting | bytes 163840 | tf_op jit(solution)/shard_map/reshape | solution.py:596
  1.2 1.1 %reshape.10.cache_lat = bf16[2,4,160,32]{3,2,1,0:T(8,128)(2,1)S(1)} reshape(bf16[2,4,5120]{2,1,0:T(4,128)(2,1)} %param.13) | data formatting | bytes 163840 | tf_op jit(solution)/shard_map/reshape | solution.py:597
  2.3 3.7 %reshape.11.w_out_hbm = bf16[9,576,96]{2,1,0:T(8,128)(2,1)} reshape(bf16[3,3,3,18432]{3,2,1,0:T(4,128)(2,1)} %param.17) | data formatting | bytes 1990656 | tf_op jit(solution)/shard_map/reshape | solution.py:650
  6.0 0.0 copy-done.5
  6.0 0.0 copy-done.3
  6.0 0.0 copy-done.6
  6.0 0.0 copy-done.4
  6.0 0.0 copy-done.2
  6.1 0.0 copy-done.1
  6.1 0.0 copy-done
  6.1 50.0 %shard_map.118.src = bf16[2,8,61440]{2,1,0:T(8,128)(2,1)} custom-call(bf16[4,2,80,64]{3,2,1,0:T(8,128)(2,1)S(1)} %reshape.9.tokens, bf16[2,4,160,32]{3,2,1,0:T(8,128)(2,1)S(1)} %reshape.10.cache_lat, bf16[2,8,192,640]{3,2,1,0:T(8,128)(2,1)} %bitcast.2, bf16[3,3,3,16,384]{4,3,2,1,0:T(8,128)(2,1)S(1)} %copy-done, bf16[3,3,192,384]{3,2,1,0:T(8,128)(2,1)} %bitcast.3, ...), custom_call_target="tpu_custom_call" | custom-call | flops 28000000000 | bytes 16000000 | tf_op jit(solution)/shard_map/pallas_call | solution.py:632
  56.1 2.5 %shard_map.119 = bf16[2,8,61440]{2,1,0:T(8,128)(2,1)} custom-call(bf16[2,8,61440]{2,1,0:T(8,128)(2,1)} %shard_map.118.src), custom_call_target="tpu_custom_call" | custom-call | tf_op jit(solution)/shard_map/pallas_call | solution.py:569
Async XLA Ops:
  0.0 6.0 %copy-start.5 = (f32[192]{0:T(256)S(1)}, f32[192]{0:T(256)}, u32[]{:S(2)}) copy-start(f32[192]{0:T(256)} %g2.1) | copy-start | bytes 2308
  0.0 6.0 %copy-start.3 = (f32[384]{0:T(512)S(1)}, f32[384]{0:T(512)}, u32[]{:S(2)}) copy-start(f32[384]{0:T(512)} %g1.1) | copy-start | bytes 4612
  0.0 6.0 %copy-start.6 = (f32[96]{0:T(128)S(1)}, f32[96]{0:T(128)}, u32[]{:S(2)}) copy-start(f32[96]{0:T(128)} %b3.1) | copy-start | bytes 1156
  0.0 6.0 %copy-start.4 = (f32[192]{0:T(256)S(1)}, f32[192]{0:T(256)}, u32[]{:S(2)}) copy-start(f32[192]{0:T(256)} %b2.1) | copy-start | bytes 2308
  0.0 6.0 %copy-start.2 = (f32[384]{0:T(512)S(1)}, f32[384]{0:T(512)}, u32[]{:S(2)}) copy-start(f32[384]{0:T(512)} %b1.1) | copy-start | bytes 4612
  0.0 6.0 %copy-start.1 = (bf16[192,96]{1,0:T(8,128)(2,1)S(1)}, bf16[192,96]{1,0:T(8,128)(2,1)}, u32[]{:S(2)}) copy-start(bf16[192,96]{1,0:T(8,128)(2,1)} %w_skip.1) | copy-start | bytes 110596
  0.0 6.0 %copy-start = (bf16[3,3,3,16,384]{4,3,2,1,0:T(8,128)(2,1)S(1)}, bf16[3,3,3,16,384]{4,3,2,1,0:T(8,128)(2,1)}, u32[]{:S(2)}) copy-start(bf16[3,3,3,16,384]{4,3,2,1,0:T(8,128)(2,1)} %w_in_hbm.1) | copy-start | bytes 995332

commit v5 on v4

--- a/solution.py
+++ b/solution.py
@@ -172,7 +172,7 @@
 
     local[2].wait()
 
-    def build_first(dt, carry):
+    def build_first(dt):
         for block in range(16):
             row_tap = ((block >> 1 & 1) + 2 * (block >> 2 & 1) + 1) % 4
             col_tap = ((block & 1) + 2 * (block >> 3) + 1) % 4
@@ -183,11 +183,11 @@
                         piece = w_in[dt, dr, dc]
                     else:
                         piece = jnp.zeros((C0, C1), BF)
-                    at = pl.ds(pl.multiple_of(dt * 256 + block * C0, C0), C0)
-                    w1[q, at, r * C1 : (r + 1) * C1] = piece
-        return carry
-
-    lax.fori_loop(0, 3, build_first, 0)
+                    at = dt * 256 + block * C0
+                    w1[q, at : at + C0, r * C1 : (r + 1) * C1] = piece
+
+    for dt in range(3):
+        build_first(dt)
 
     partners = 5 - 2 * top.astype(jnp.int32) - 2 * bottom.astype(jnp.int32)
     pl.semaphore_wait(barrier, partners)
@@ -232,12 +232,9 @@
             )
             ref[t, row] = pair.astype(BF)
 
-    def cached_own(t, carry):
+    for t in range(2):
         for row in range(1, 9):
             cached_row(t, row, cf[t, row - 1])
-        return carry
-
-    lax.fori_loop(0, 2, cached_own, 0)
 
     local[3].wait()
     taps = {(0, 0): (0, 1), (1, 0): (2,), (0, 1): (0,), (1, 1): (1, 2)}
@@ -309,18 +306,6 @@
 
     def all_windows(t, get, base):
         windows(t + base, [get(t, u) for u in range(4)], range(4))
-
-    def each_frame(work):
-        def cached_frame(t, carry):
-            work(t, cached_rows, 0)
-            return carry
-
-        def token_frame(t, carry):
-            work(t, token_rows, 2)
-            return carry
-
-        lax.fori_loop(0, 2, cached_frame, 0)
-        lax.fori_loop(0, 4, token_frame, 0)
 
     keep_top = jnp.where(top, 0.0, 1.0)
     keep_bottom = jnp.where(bottom, 0.0, 1.0)
@@ -422,7 +407,10 @@
         for at, i in enumerate((0, 1, 3, 4)):
             second_finish(f, i, at, held)
 
-    each_frame(inner_windows)
+    for t in range(2):
+        inner_windows(t, cached_rows, 0)
+    for t in range(4):
+        inner_windows(t, token_rows, 2)
     first(2)
     first(3)
     second_products(slice(0, 4), ((2, 3),), 4 * WIDE, 4 * PATCH_COLS, (y2e, y2o))

time: 59 us -> 58.2 us (0.986)
  Pallas kernels: 52.4 us -> 51.7 us
    pallas_call x1, Pallas kernels: 50 us -> 49.3 us  [shards(): pl.pallas_call(kernel, out_shape=jax.ShapeDtypeStruct((2, 8, 640 * C3), B...]
where the time goes in v5:
time: 58.2 us; the launch traced here: 58 us
  Pallas kernels  51.7 us (89%)
  local copies, waits for them, and re-layouts  5.99 us (10%)
    pallas_call x1, Pallas kernels, shards(): pl.pallas_call(kernel, out_shape=jax.ShapeDtypeStruct((2, 8, 640 * C3), B...  49.3 us
    reshape x1, local copies, waits for them, and re-layouts, shards(): weight_out.reshape(9, 3 * C2, C3)  3.73 us
    pallas_call x1, Pallas kernels, copied(): pl.pallas_call(body, out_shape=jax.ShapeDtypeStruct(x.shape, x.dtype), in...  2.47 us

profile of v5, /device:TPU:24, one launch (start us, length us, event | category | flops | bytes accessed | tf_op | source)
XLA Modules:
  0.0 58.0 jit_solution(266838594015860600)
XLA Ops:
  0.0 0.0 copy-start.5
  0.0 0.0 copy-start.3
  0.0 0.0 copy-start.6
  0.0 0.0 copy-start.4
  0.0 0.0 copy-start.2
  0.0 0.0 copy-start.1
  0.0 0.0 copy-start
  0.0 1.1 %reshape.9.tokens = bf16[4,2,80,64]{3,2,1,0:T(8,128)(2,1)S(1)} reshape(bf16[4,2,5120]{2,1,0:T(2,128)(2,1)} %param.12) | data formatting | bytes 163840 | tf_op jit(solution)/shard_map/reshape | solution.py:584
  1.2 1.1 %reshape.10.cache_lat = bf16[2,4,160,32]{3,2,1,0:T(8,128)(2,1)S(1)} reshape(bf16[2,4,5120]{2,1,0:T(4,128)(2,1)} %param.13) | data formatting | bytes 163840 | tf_op jit(solution)/shard_map/reshape | solution.py:585
  2.3 3.7 %reshape.11.w_out_hbm = bf16[9,576,96]{2,1,0:T(8,128)(2,1)} reshape(bf16[3,3,3,18432]{3,2,1,0:T(4,128)(2,1)} %param.17) | data formatting | bytes 1990656 | tf_op jit(solution)/shard_map/reshape | solution.py:638
  6.0 0.0 copy-done.5
  6.0 0.0 copy-done.3
  6.0 0.0 copy-done.6
  6.0 0.0 copy-done.4
  6.0 0.0 copy-done.2
  6.1 0.0 copy-done.1
  6.1 0.0 copy-done
  6.1 49.3 %shard_map.118.src = bf16[2,8,61440]{2,1,0:T(8,128)(2,1)} custom-call(bf16[4,2,80,64]{3,2,1,0:T(8,128)(2,1)S(1)} %reshape.9.tokens, bf16[2,4,160,32]{3,2,1,0:T(8,128)(2,1)S(1)} %reshape.10.cache_lat, bf16[2,8,192,640]{3,2,1,0:T(8,128)(2,1)} %bitcast.2, bf16[3,3,3,16,384]{4,3,2,1,0:T(8,128)(2,1)S(1)} %copy-done, bf16[3,3,192,384]{3,2,1,0:T(8,128)(2,1)} %bitcast.3, ...), custom_call_target="tpu_custom_call" | custom-call | flops 28000000000 | bytes 16000000 | tf_op jit(solution)/shard_map/pallas_call | solution.py:620
  55.3 2.5 %shard_map.119 = bf16[2,8,61440]{2,1,0:T(8,128)(2,1)} custom-call(bf16[2,8,61440]{2,1,0:T(8,128)(2,1)} %shard_map.118.src), custom_call_target="tpu_custom_call" | custom-call | tf_op jit(solution)/shard_map/pallas_call | solution.py:557
Async XLA Ops:
  0.0 6.0 %copy-start.5 = (f32[192]{0:T(256)S(1)}, f32[192]{0:T(256)}, u32[]{:S(2)}) copy-start(f32[192]{0:T(256)} %g2.1) | copy-start | bytes 2308
  0.0 6.0 %copy-start.3 = (f32[384]{0:T(512)S(1)}, f32[384]{0:T(512)}, u32[]{:S(2)}) copy-start(f32[384]{0:T(512)} %g1.1) | copy-start | bytes 4612
  0.0 6.0 %copy-start.6 = (f32[96]{0:T(128)S(1)}, f32[96]{0:T(128)}, u32[]{:S(2)}) copy-start(f32[96]{0:T(128)} %b3.1) | copy-start | bytes 1156
  0.0 6.0 %copy-start.4 = (f32[192]{0:T(256)S(1)}, f32[192]{0:T(256)}, u32[]{:S(2)}) copy-start(f32[192]{0:T(256)} %b2.1) | copy-start | bytes 2308
  0.0 6.0 %copy-start.2 = (f32[384]{0:T(512)S(1)}, f32[384]{0:T(512)}, u32[]{:S(2)}) copy-start(f32[384]{0:T(512)} %b1.1) | copy-start | bytes 4612
  0.0 6.0 %copy-start.1 = (bf16[192,96]{1,0:T(8,128)(2,1)S(1)}, bf16[192,96]{1,0:T(8,128)(2,1)}, u32[]{:S(2)}) copy-start(bf16[192,96]{1,0:T(8,128)(2,1)} %w_skip.1) | copy-start | bytes 110596
  0.0 6.0 %copy-start = (bf16[3,3,3,16,384]{4,3,2,1,0:T(8,128)(2,1)S(1)}, bf16[3,3,3,16,384]{4,3,2,1,0:T(8,128)(2,1)}, u32[]{:S(2)}) copy-start(bf16[3,3,3,16,384]{4,3,2,1,0:T(8,128)(2,1)} %w_in_hbm.1) | copy-start | bytes 995332
